TPU v7x, 32 devices: a whole 2x2x4 slice. The times are simulated.
32 devices in a mesh: fsdp: 16 (over z, y, core), sp: 2 (over x).
Axes of the slice: x: 2, y: 2, z: 4, core: 2. Of those that a mesh axis runs over, the one named last changes fastest.
Arguments:
- hidden_in: bfloat16 [32, 2048, 512], P('fsdp', 'sp'), may hold values from -6 to 6
- token_stream: bfloat16 [32, 2048, 512], P('fsdp', 'sp'), may hold values from -6 to 6
- encoder_out: bfloat16 [32, 1024, 512], P('fsdp', 'sp'), may hold values from -6 to 6
- out_grad: bfloat16 [32, 2048, 512], P('fsdp', 'sp'), may hold values from -6 to 6
- doc_ids: int32 [32, 8], P('fsdp'), may hold values from 0 to 3, never falling along the last dimension, each value on 1 to 4 neighbouring positions
- key_order: int32 [32, 8, 256], P('fsdp'), may hold values from 0 to 255, each once within a row
- context_size: int32 [32, 8, 256], P('fsdp'), may hold values from 2 to 256
- self_query: bfloat16 [512, 512], P('fsdp'), may hold values from -0.375 to 0.375
- self_key: bfloat16 [512, 512], P('fsdp'), may hold values from -0.25 to 0.25
- self_value: bfloat16 [512, 512], P('fsdp'), may hold values from -0.25 to 0.25
- self_output: bfloat16 [512, 512], P('fsdp'), may hold values from -1.5 to 1.5
- cross_query: bfloat16 [512, 512], P('fsdp'), may hold values from -0.375 to 0.375
- cross_key: bfloat16 [512, 512], P('fsdp'), may hold values from -0.25 to 0.25
- cross_value: bfloat16 [512, 512], P('fsdp'), may hold values from -0.25 to 0.25
- cross_output: bfloat16 [512, 512], P('fsdp'), may hold values from -3 to 3
- inner_weight: bfloat16 [512, 2048], P('fsdp'), may hold values from -0.25 to 0.25
- inner_bias: bfloat16 [2048], P('fsdp'), may hold values from -3 to 3
- outer_weight: bfloat16 [2048, 512], P('fsdp'), may hold values from -0.1875 to 0.1875
- outer_bias: bfloat16 [512], P('fsdp'), may hold values from -3 to 3
- first_gain: bfloat16 [512], P('fsdp'), may hold values from 0.25 to 1.75
- first_shift: bfloat16 [512], P('fsdp'), may hold values from -2 to 2
- second_gain: bfloat16 [512], P('fsdp'), may hold values from 0.25 to 1.75
- second_shift: bfloat16 [512], P('fsdp'), may hold values from -2 to 2
- third_gain: bfloat16 [512], P('fsdp'), may hold values from 0.25 to 1.75
- third_shift: bfloat16 [512], P('fsdp'), may hold values from -2 to 2
Outputs:
- layer_out: float32 [32, 2048, 512], P('fsdp', 'sp')
- hidden_grad: float32 [32, 2048, 512], P('fsdp', 'sp')
- token_grad: float32 [32, 2048, 512], P('fsdp', 'sp')
- encoder_grad: float32 [32, 1024, 512], P('fsdp', 'sp')
- self_query_grad: float32 [512, 512], P('fsdp')
- self_key_grad: float32 [512, 512], P('fsdp')
- self_value_grad: float32 [512, 512], P('fsdp')
- self_output_grad: float32 [512, 512], P('fsdp')
- cross_query_grad: float32 [512, 512], P('fsdp')
- cross_key_grad: float32 [512, 512], P('fsdp')
- cross_value_grad: float32 [512, 512], P('fsdp')
- cross_output_grad: float32 [512, 512], P('fsdp')
- inner_weight_grad: float32 [512, 2048], P('fsdp')
- inner_bias_grad: float32 [2048], P('fsdp')
- outer_weight_grad: float32 [2048, 512], P('fsdp')
- outer_bias_grad: float32 [512], P('fsdp')
- first_gain_grad: float32 [512], P('fsdp')
- first_shift_grad: float32 [512], P('fsdp')
- second_gain_grad: float32 [512], P('fsdp')
- second_shift_grad: float32 [512], P('fsdp')
- third_gain_grad: float32 [512], P('fsdp')
- third_shift_grad: float32 [512], P('fsdp')
Inputs may be any that keep to these rules, and one draw needn't show every extreme that they name: `doc_ids`: block ids never fall along a sequence's 8 blocks; tokens may attend only within blocks of equal id. `key_order`: the 256 entries of each block are a permutation.
All inputs are finite; a program needn't handle non-finite values.
Results may differ from a plain program's by a relative error of at most 0.03.
Values may be sent and summed in bfloat16 or wider, within the bound.
No kernel may reach another device: no remote copies, remote signals or barrier semaphores. Data moves between devices by JAX's collectives and lax.ppermute only.
A program may use at most 256 MiB of HBM per device.

v0:
```python
import math

import jax
import jax.numpy as jnp
from jax import lax
from jax.sharding import PartitionSpec as P

HD = 64


epsilon = 1e-05
mask_fill = -1000000000.0


def matmul(left, right):
    return jnp.dot(left, right, preferred_element_type=jnp.float32)


def left_product(left, right):
    return lax.dot_general(
        left, right, (((0,), (0,)), ((), ())), preferred_element_type=jnp.float32
    )


def right_product(left, right):
    return lax.dot_general(
        left, right, (((1,), (1,)), ((), ())), preferred_element_type=jnp.float32
    )


def smooth_gate(values):
    return jax.nn.gelu(values, approximate=False)


def normalize(rows, gain, shift):
    center = rows - jnp.mean(rows, axis=-1, keepdims=True)
    scaled = center * lax.rsqrt(jnp.mean(center * center, axis=-1, keepdims=True) + epsilon)
    return scaled * gain + shift


def normalize_back(rows, gain, upstream):
    center = rows - jnp.mean(rows, axis=-1, keepdims=True)
    inverse = lax.rsqrt(jnp.mean(center * center, axis=-1, keepdims=True) + epsilon)
    scaled = center * inverse
    through = upstream * gain
    row_grad = inverse * (
        through
        - jnp.mean(through, axis=-1, keepdims=True)
        - scaled * jnp.mean(through * scaled, axis=-1, keepdims=True)
    )
    return (row_grad, jnp.sum(upstream * scaled, axis=0), jnp.sum(upstream, axis=0))


def no_mask(seq_index, row_start, block_rows):
    return None


def attend_forward(query, key_rows, value_rows, allow_fn):
    seq_count, length, model_width = query.shape
    key_count = key_rows.shape[1]
    head_count = model_width // HD
    block_rows = min(512, length)
    block_count = length // block_rows
    score_scale = 1.0 / math.sqrt(HD)

    def attend_one_block(flat_index):
        seq_index = flat_index // block_count
        row_start = flat_index % block_count * block_rows
        query_seq = lax.dynamic_index_in_dim(query, seq_index, 0, False)
        query_part = lax.dynamic_slice_in_dim(query_seq, row_start, block_rows, 0).reshape(
            block_rows, head_count, HD
        )
        key_part = lax.dynamic_index_in_dim(key_rows, seq_index, 0, False).reshape(
            key_count, head_count, HD
        )
        value_part = lax.dynamic_index_in_dim(value_rows, seq_index, 0, False).reshape(
            key_count, head_count, HD
        )
        scores = (
            jnp.einsum("qhd,khd->hqk", query_part, key_part, preferred_element_type=jnp.float32)
            * score_scale
        )
        allowed = allow_fn(seq_index, row_start, block_rows)
        if allowed is not None:
            scores = jnp.where(allowed[None], scores, mask_fill)
        row_max = jnp.max(scores, axis=-1, keepdims=True)
        exp_terms = jnp.exp(scores - row_max)
        if allowed is not None:
            exp_terms = jnp.where(allowed[None], exp_terms, 0.0)
        row_total = jnp.sum(exp_terms, axis=-1, keepdims=True)
        prob_rows = (exp_terms / row_total).astype(jnp.bfloat16)
        mixed_rows = jnp.einsum(
            "hqk,khd->qhd", prob_rows, value_part, preferred_element_type=jnp.float32
        )
        return (
            mixed_rows.reshape(block_rows, model_width).astype(jnp.bfloat16),
            (row_max + jnp.log(row_total))[..., 0],
        )

    mixed_heads, log_total = lax.map(
        attend_one_block, jnp.arange(seq_count * block_count, dtype=jnp.int32)
    )
    return (mixed_heads.reshape(seq_count, length, model_width), log_total)


def attend_backward(query, key_rows, value_rows, mixed_grad, log_total, allow_fn):
    seq_count, length, model_width = query.shape
    key_count = key_rows.shape[1]
    head_count = model_width // HD
    block_rows = min(512, length)
    block_count = length // block_rows
    score_scale = 1.0 / math.sqrt(HD)

    def one_sequence(seq_index):
        query_seq = lax.dynamic_index_in_dim(query, seq_index, 0, False)
        grad_seq = lax.dynamic_index_in_dim(mixed_grad, seq_index, 0, False)
        key_part = lax.dynamic_index_in_dim(key_rows, seq_index, 0, False).reshape(
            key_count, head_count, HD
        )
        value_part = lax.dynamic_index_in_dim(value_rows, seq_index, 0, False).reshape(
            key_count, head_count, HD
        )

        def one_one_block(carried, block_index):
            key_acc, value_acc = carried
            row_start = block_index * block_rows
            query_part = lax.dynamic_slice_in_dim(query_seq, row_start, block_rows, 0).reshape(
                block_rows, head_count, HD
            )
            grad_part = lax.dynamic_slice_in_dim(grad_seq, row_start, block_rows, 0).reshape(
                block_rows, head_count, HD
            )
            block_total = lax.dynamic_index_in_dim(
                log_total, seq_index * block_count + block_index, 0, False
            )
            scores = (
                jnp.einsum("qhd,khd->hqk", query_part, key_part, preferred_element_type=jnp.float32)
                * score_scale
            )
            allowed = allow_fn(seq_index, row_start, block_rows)
            if allowed is not None:
                scores = jnp.where(allowed[None], scores, mask_fill)
            prob_rows = jnp.exp(scores - block_total[..., None])
            if allowed is not None:
                prob_rows = jnp.where(allowed[None], prob_rows, 0.0)
            prob_grad = jnp.einsum(
                "qhd,khd->hqk", grad_part, value_part, preferred_element_type=jnp.float32
            )
            row_inner = jnp.sum(prob_rows * prob_grad, axis=-1, keepdims=True)
            score_grad = (prob_rows * (prob_grad - row_inner)).astype(jnp.bfloat16)
            query_grad = (
                jnp.einsum("hqk,khd->qhd", score_grad, key_part, preferred_element_type=jnp.float32)
                * score_scale
            )
            key_acc = (
                key_acc
                + jnp.einsum(
                    "hqk,qhd->khd", score_grad, query_part, preferred_element_type=jnp.float32
                )
                * score_scale
            )
            value_acc = value_acc + jnp.einsum(
                "hqk,qhd->khd",
                prob_rows.astype(jnp.bfloat16),
                grad_part,
                preferred_element_type=jnp.float32,
            )
            return (
                (key_acc, value_acc),
                query_grad.reshape(block_rows, model_width).astype(jnp.bfloat16),
            )

        zero_keys = jnp.zeros((key_count, head_count, HD), jnp.float32)
        (key_acc, value_acc), query_grads = lax.scan(
            one_one_block, (zero_keys, zero_keys), jnp.arange(block_count, dtype=jnp.int32)
        )
        return (
            query_grads.reshape(length, model_width),
            key_acc.reshape(key_count, model_width).astype(jnp.bfloat16),
            value_acc.reshape(key_count, model_width).astype(jnp.bfloat16),
        )

    return lax.map(one_sequence, jnp.arange(seq_count, dtype=jnp.int32))


def on_device(
    hidden_in,
    token_stream,
    encoder_out,
    out_grad,
    doc_ids,
    key_order,
    context_size,
    self_query,
    self_key,
    self_value,
    self_output,
    cross_query,
    cross_key,
    cross_value,
    cross_output,
    inner_weight,
    inner_bias,
    outer_weight,
    outer_bias,
    first_gain,
    first_shift,
    second_gain,
    second_shift,
    third_gain,
    third_shift,
):
    (
        w_query,
        w_key,
        w_value,
        w_output,
        c_query,
        c_key,
        c_value,
        c_output,
        w_inner,
        b_inner,
        w_outer,
        b_outer,
        g_first,
        s_first,
        g_second,
        s_second,
        g_third,
        s_third,
    ) = (
        lax.all_gather(self_query, "fsdp", axis=0, tiled=True),
        lax.all_gather(self_key, "fsdp", axis=0, tiled=True),
        lax.all_gather(self_value, "fsdp", axis=0, tiled=True),
        lax.all_gather(self_output, "fsdp", axis=0, tiled=True),
        lax.all_gather(cross_query, "fsdp", axis=0, tiled=True),
        lax.all_gather(cross_key, "fsdp", axis=0, tiled=True),
        lax.all_gather(cross_value, "fsdp", axis=0, tiled=True),
        lax.all_gather(cross_output, "fsdp", axis=0, tiled=True),
        lax.all_gather(inner_weight, "fsdp", axis=0, tiled=True),
        lax.all_gather(inner_bias, "fsdp", axis=0, tiled=True),
        lax.all_gather(outer_weight, "fsdp", axis=0, tiled=True),
        lax.all_gather(outer_bias, "fsdp", axis=0, tiled=True),
        lax.all_gather(first_gain, "fsdp", axis=0, tiled=True),
        lax.all_gather(first_shift, "fsdp", axis=0, tiled=True),
        lax.all_gather(second_gain, "fsdp", axis=0, tiled=True),
        lax.all_gather(second_shift, "fsdp", axis=0, tiled=True),
        lax.all_gather(third_gain, "fsdp", axis=0, tiled=True),
        lax.all_gather(third_shift, "fsdp", axis=0, tiled=True),
    )
    seq_count, local_len, model_width = hidden_in.shape
    enc_len = encoder_out.shape[1]
    hid_rows = hidden_in.reshape(-1, model_width)
    tok_rows = token_stream.reshape(-1, model_width)
    enc_rows = encoder_out.reshape(-1, model_width)
    block_len = key_order.shape[2]
    tok_doc = jnp.repeat(doc_ids, block_len, axis=1)
    tok_order = key_order.reshape(seq_count, -1)
    tok_reach = context_size.reshape(seq_count, -1)
    key_places = jnp.arange(tok_doc.shape[1], dtype=jnp.int32)

    def self_allow(seq_index, row_start, block_rows):
        doc_row = lax.dynamic_index_in_dim(tok_doc, seq_index, 0, False)
        order_row = lax.dynamic_index_in_dim(tok_order, seq_index, 0, False)
        reach_row = lax.dynamic_index_in_dim(tok_reach, seq_index, 0, False)
        query_doc = lax.dynamic_slice_in_dim(doc_row, row_start, block_rows)
        query_reach = lax.dynamic_slice_in_dim(reach_row, row_start, block_rows)
        query_places = row_start + jnp.arange(block_rows, dtype=jnp.int32)
        return (
            (query_doc[:, None] == doc_row[None, :])
            & (order_row[None, :] < query_reach[:, None])
            & (query_places[:, None] != key_places[None, :])
        )

    q_self = (
        matmul(hid_rows, w_query).astype(jnp.bfloat16).reshape(seq_count, local_len, model_width)
    )
    k_self = matmul(tok_rows, w_key).astype(jnp.bfloat16).reshape(seq_count, local_len, model_width)
    v_self = (
        matmul(tok_rows, w_value).astype(jnp.bfloat16).reshape(seq_count, local_len, model_width)
    )
    q_heads, k_heads, v_heads = (
        lax.all_to_all(q_self, "sp", split_axis=2, concat_axis=1, tiled=True),
        lax.all_to_all(k_self, "sp", split_axis=2, concat_axis=1, tiled=True),
        lax.all_to_all(v_self, "sp", split_axis=2, concat_axis=1, tiled=True),
    )
    self_heads, self_total = attend_forward(q_heads, k_heads, v_heads, self_allow)
    self_tok = lax.all_to_all(self_heads, "sp", split_axis=1, concat_axis=2, tiled=True).reshape(
        -1, model_width
    )
    first_sum = hid_rows.astype(jnp.float32) + matmul(self_tok, w_output)
    normed = normalize(first_sum, g_first.astype(jnp.float32), s_first.astype(jnp.float32))
    normed_low = normed.astype(jnp.bfloat16)
    q_cross = (
        matmul(normed_low, c_query).astype(jnp.bfloat16).reshape(seq_count, local_len, model_width)
    )
    k_cross = matmul(enc_rows, c_key).astype(jnp.bfloat16).reshape(seq_count, enc_len, model_width)
    v_cross = (
        matmul(enc_rows, c_value).astype(jnp.bfloat16).reshape(seq_count, enc_len, model_width)
    )
    cq_heads, ck_heads, cv_heads = (
        lax.all_to_all(q_cross, "sp", split_axis=2, concat_axis=1, tiled=True),
        lax.all_to_all(k_cross, "sp", split_axis=2, concat_axis=1, tiled=True),
        lax.all_to_all(v_cross, "sp", split_axis=2, concat_axis=1, tiled=True),
    )
    cross_heads, cross_total = attend_forward(cq_heads, ck_heads, cv_heads, no_mask)
    cross_tok = lax.all_to_all(cross_heads, "sp", split_axis=1, concat_axis=2, tiled=True).reshape(
        -1, model_width
    )
    second_sum = normed + matmul(cross_tok, c_output)
    middle = normalize(second_sum, g_second.astype(jnp.float32), s_second.astype(jnp.float32))
    middle_low = middle.astype(jnp.bfloat16)
    inner_pre = matmul(middle_low, w_inner) + b_inner.astype(jnp.float32)
    gate_value, gate_pull = jax.vjp(smooth_gate, inner_pre)
    active = gate_value.astype(jnp.bfloat16)
    third_sum = middle + matmul(active, w_outer) + b_outer.astype(jnp.float32)
    result = normalize(third_sum, g_third.astype(jnp.float32), s_third.astype(jnp.float32))
    layer_out = result.reshape(seq_count, local_len, model_width)
    upstream = out_grad.reshape(-1, model_width).astype(jnp.float32)
    third_grad, g_third_grad, s_third_grad = normalize_back(
        third_sum, g_third.astype(jnp.float32), upstream
    )
    outer_low = third_grad.astype(jnp.bfloat16)
    w_outer_grad = left_product(active, outer_low)
    b_outer_grad = jnp.sum(outer_low.astype(jnp.float32), axis=0)
    active_grad = right_product(outer_low, w_outer)
    inner_low = gate_pull(active_grad)[0].astype(jnp.bfloat16)
    w_inner_grad = left_product(middle_low, inner_low)
    b_inner_grad = jnp.sum(inner_low.astype(jnp.float32), axis=0)
    middle_grad = third_grad + right_product(inner_low, w_inner)
    second_grad, g_second_grad, s_second_grad = normalize_back(
        second_sum, g_second.astype(jnp.float32), middle_grad
    )
    cross_low = second_grad.astype(jnp.bfloat16)
    c_output_grad = left_product(cross_tok, cross_low)
    cross_mixed = (
        right_product(cross_low, c_output)
        .astype(jnp.bfloat16)
        .reshape(seq_count, local_len, model_width)
    )
    cross_mixed_heads = lax.all_to_all(cross_mixed, "sp", split_axis=2, concat_axis=1, tiled=True)
    cq_grad, ck_grad, cv_grad = attend_backward(
        cq_heads, ck_heads, cv_heads, cross_mixed_heads, cross_total, no_mask
    )
    cq_tok, ck_tok, cv_tok = (
        lax.all_to_all(cq_grad, "sp", split_axis=1, concat_axis=2, tiled=True),
        lax.all_to_all(ck_grad, "sp", split_axis=1, concat_axis=2, tiled=True),
        lax.all_to_all(cv_grad, "sp", split_axis=1, concat_axis=2, tiled=True),
    )
    cq_tok = cq_tok.reshape(-1, model_width)
    ck_tok = ck_tok.reshape(-1, model_width)
    cv_tok = cv_tok.reshape(-1, model_width)
    c_query_grad = left_product(normed_low, cq_tok)
    c_key_grad = left_product(enc_rows, ck_tok)
    c_value_grad = left_product(enc_rows, cv_tok)
    encoder_grad = right_product(ck_tok, c_key) + right_product(cv_tok, c_value)
    normed_grad = second_grad + right_product(cq_tok, c_query)
    first_grad, g_first_grad, s_first_grad = normalize_back(
        first_sum, g_first.astype(jnp.float32), normed_grad
    )
    self_low = first_grad.astype(jnp.bfloat16)
    w_output_grad = left_product(self_tok, self_low)
    self_mixed = (
        right_product(self_low, w_output)
        .astype(jnp.bfloat16)
        .reshape(seq_count, local_len, model_width)
    )
    self_mixed_heads = lax.all_to_all(self_mixed, "sp", split_axis=2, concat_axis=1, tiled=True)
    q_grad, k_grad, v_grad = attend_backward(
        q_heads, k_heads, v_heads, self_mixed_heads, self_total, self_allow
    )
    q_tok, k_tok, v_tok = (
        lax.all_to_all(q_grad, "sp", split_axis=1, concat_axis=2, tiled=True),
        lax.all_to_all(k_grad, "sp", split_axis=1, concat_axis=2, tiled=True),
        lax.all_to_all(v_grad, "sp", split_axis=1, concat_axis=2, tiled=True),
    )
    q_tok = q_tok.reshape(-1, model_width)
    k_tok = k_tok.reshape(-1, model_width)
    v_tok = v_tok.reshape(-1, model_width)
    w_query_grad = left_product(hid_rows, q_tok)
    w_key_grad = left_product(tok_rows, k_tok)
    w_value_grad = left_product(tok_rows, v_tok)
    hidden_grad = first_grad + right_product(q_tok, w_query)
    token_grad = right_product(k_tok, w_key) + right_product(v_tok, w_value)
    pieces = (
        lax.psum_scatter(
            w_query_grad.astype(jnp.bfloat16), "fsdp", scatter_dimension=0, tiled=True
        ).astype(jnp.float32),
        lax.psum_scatter(
            w_key_grad.astype(jnp.bfloat16), "fsdp", scatter_dimension=0, tiled=True
        ).astype(jnp.float32),
        lax.psum_scatter(
            w_value_grad.astype(jnp.bfloat16), "fsdp", scatter_dimension=0, tiled=True
        ).astype(jnp.float32),
        lax.psum_scatter(
            w_output_grad.astype(jnp.bfloat16), "fsdp", scatter_dimension=0, tiled=True
        ).astype(jnp.float32),
        lax.psum_scatter(
            c_query_grad.astype(jnp.bfloat16), "fsdp", scatter_dimension=0, tiled=True
        ).astype(jnp.float32),
        lax.psum_scatter(
            c_key_grad.astype(jnp.bfloat16), "fsdp", scatter_dimension=0, tiled=True
        ).astype(jnp.float32),
        lax.psum_scatter(
            c_value_grad.astype(jnp.bfloat16), "fsdp", scatter_dimension=0, tiled=True
        ).astype(jnp.float32),
        lax.psum_scatter(
            c_output_grad.astype(jnp.bfloat16), "fsdp", scatter_dimension=0, tiled=True
        ).astype(jnp.float32),
        lax.psum_scatter(
            w_inner_grad.astype(jnp.bfloat16), "fsdp", scatter_dimension=0, tiled=True
        ).astype(jnp.float32),
        lax.psum_scatter(
            b_inner_grad.astype(jnp.bfloat16), "fsdp", scatter_dimension=0, tiled=True
        ).astype(jnp.float32),
        lax.psum_scatter(
            w_outer_grad.astype(jnp.bfloat16), "fsdp", scatter_dimension=0, tiled=True
        ).astype(jnp.float32),
        lax.psum_scatter(
            b_outer_grad.astype(jnp.bfloat16), "fsdp", scatter_dimension=0, tiled=True
        ).astype(jnp.float32),
        lax.psum_scatter(
            g_first_grad.astype(jnp.bfloat16), "fsdp", scatter_dimension=0, tiled=True
        ).astype(jnp.float32),
        lax.psum_scatter(
            s_first_grad.astype(jnp.bfloat16), "fsdp", scatter_dimension=0, tiled=True
        ).astype(jnp.float32),
        lax.psum_scatter(
            g_second_grad.astype(jnp.bfloat16), "fsdp", scatter_dimension=0, tiled=True
        ).astype(jnp.float32),
        lax.psum_scatter(
            s_second_grad.astype(jnp.bfloat16), "fsdp", scatter_dimension=0, tiled=True
        ).astype(jnp.float32),
        lax.psum_scatter(
            g_third_grad.astype(jnp.bfloat16), "fsdp", scatter_dimension=0, tiled=True
        ).astype(jnp.float32),
        lax.psum_scatter(
            s_third_grad.astype(jnp.bfloat16), "fsdp", scatter_dimension=0, tiled=True
        ).astype(jnp.float32),
    )
    reduced = (
        lax.psum(pieces[0].astype(jnp.bfloat16), "sp").astype(jnp.float32),
        lax.psum(pieces[1].astype(jnp.bfloat16), "sp").astype(jnp.float32),
        lax.psum(pieces[2].astype(jnp.bfloat16), "sp").astype(jnp.float32),
        lax.psum(pieces[3].astype(jnp.bfloat16), "sp").astype(jnp.float32),
        lax.psum(pieces[4].astype(jnp.bfloat16), "sp").astype(jnp.float32),
        lax.psum(pieces[5].astype(jnp.bfloat16), "sp").astype(jnp.float32),
        lax.psum(pieces[6].astype(jnp.bfloat16), "sp").astype(jnp.float32),
        lax.psum(pieces[7].astype(jnp.bfloat16), "sp").astype(jnp.float32),
        lax.psum(pieces[8].astype(jnp.bfloat16), "sp").astype(jnp.float32),
        lax.psum(pieces[9].astype(jnp.bfloat16), "sp").astype(jnp.float32),
        lax.psum(pieces[10].astype(jnp.bfloat16), "sp").astype(jnp.float32),
        lax.psum(pieces[11].astype(jnp.bfloat16), "sp").astype(jnp.float32),
        lax.psum(pieces[12].astype(jnp.bfloat16), "sp").astype(jnp.float32),
        lax.psum(pieces[13].astype(jnp.bfloat16), "sp").astype(jnp.float32),
        lax.psum(pieces[14].astype(jnp.bfloat16), "sp").astype(jnp.float32),
        lax.psum(pieces[15].astype(jnp.bfloat16), "sp").astype(jnp.float32),
        lax.psum(pieces[16].astype(jnp.bfloat16), "sp").astype(jnp.float32),
        lax.psum(pieces[17].astype(jnp.bfloat16), "sp").astype(jnp.float32),
    )
    return (
        layer_out,
        hidden_grad.reshape(seq_count, local_len, model_width),
        token_grad.reshape(seq_count, local_len, model_width),
        encoder_grad.reshape(seq_count, enc_len, model_width),
        reduced[0],
        reduced[1],
        reduced[2],
        reduced[3],
        reduced[4],
        reduced[5],
        reduced[6],
        reduced[7],
        reduced[8],
        reduced[9],
        reduced[10],
        reduced[11],
        reduced[12],
        reduced[13],
        reduced[14],
        reduced[15],
        reduced[16],
        reduced[17],
    )


def solution(mesh):
    return jax.shard_map(
        on_device,
        mesh=mesh,
        in_specs=(
            P("fsdp", "sp", None),
            P("fsdp", "sp", None),
            P("fsdp", "sp", None),
            P("fsdp", "sp", None),
            P("fsdp", None),
            P("fsdp", None, None),
            P("fsdp", None, None),
            P("fsdp", None),
            P("fsdp", None),
            P("fsdp", None),
            P("fsdp", None),
            P("fsdp", None),
            P("fsdp", None),
            P("fsdp", None),
            P("fsdp", None),
            P("fsdp", None),
            P("fsdp"),
            P("fsdp", None),
            P("fsdp"),
            P("fsdp"),
            P("fsdp"),
            P("fsdp"),
            P("fsdp"),
            P("fsdp"),
            P("fsdp"),
        ),
        out_specs=(
            P("fsdp", "sp", None),
            P("fsdp", "sp", None),
            P("fsdp", "sp", None),
            P("fsdp", "sp", None),
            P("fsdp", None),
            P("fsdp", None),
            P("fsdp", None),
            P("fsdp", None),
            P("fsdp", None),
            P("fsdp", None),
            P("fsdp", None),
            P("fsdp", None),
            P("fsdp", None),
            P("fsdp"),
            P("fsdp", None),
            P("fsdp"),
            P("fsdp"),
            P("fsdp"),
            P("fsdp"),
            P("fsdp"),
            P("fsdp"),
            P("fsdp"),
        ),
        check_vma=False,
    )
```

profile of v0, /device:TPU:0, one launch (start us, length us, event | category | flops | bytes accessed | tf_op | source)
XLA Modules:
  0.0 2422.4 jit_solution(14643364429011673969)
XLA Ops:
  7.2 24.9 %all_gather.54 = bf16[512,512]{1,0:T(8,128)(2,1)S(1)} all-gather(bf16[32,512]{1,0:T(8,128)(2,1)} %param.46), channel_id=1, replica_groups=mesh['fsdp'=16,'sp'=2] {'fsdp'}, dimensions={0}, use_global_device_ids=true | all-gather | bytes 557056 | tf_op jit(solution)/shard_map/all_gather | solution.py:235
  45.7 18.9 all_gather.56
  78.3 20.2 all_gather.55
  114.2 20.8 all_gather.60
  165.1 191.0 %while.118 = (s32[]{:T(128)}, bf16[8,512,256]{2,1,0:T(8,128)(2,1)}, f32[8,4,512]{2,1,0:T(4,128)S(1)}, s32[8]{0:T(128)S(1)}, bf16[2,2048,256]{1,2,0:T(8,128)(2,1)...) while((s32[]{:T(128)}, bf16[8,512,256]{2,1,0:T(8,128)(2,1)}, ...), condition=%wide.region_3.4_spmd.clone, body=%wide.region_0.3_spmd.clone.sunk | while | flops 1137834496 | bytes 67240992 | solution.py:100
  372.7 32.1 %all-reduce.16 = (bf16[512]{0:T(512)(128)(2,1)S(1)}, bf16[512]{0:T(512)(128)(2,1)S(1)}, bf16[512]{0:T(512)(128)(2,1)S(1)}, bf16[512]{0:T(512)(128)(2,1)S(1)}, bf...) all-reduce(bf16[512]{0:T(512)(128)(2,1)S(1)} %dynamic-update-slice.1,, ...), channel_id=1, replica_groups=mesh['fsdp'=16,'sp'=2] {'fsdp'}, use_global_device_ids=true, to_apply=%add.1 | all-reduce | flops 3072 | bytes 12288
  408.5 18.7 all_gather.62
  432.1 20.5 all_gather.57
  452.5 20.3 all_gather.61
  549.6 96.6 %while.115 = (s32[]{:T(128)}, bf16[8,512,256]{2,1,0:T(8,128)(2,1)}, f32[8,4,512]{2,1,0:T(4,128)S(1)}, s32[8]{0:T(128)S(1)}, bf16[2,1024,256]{1,2,0:T(8,128)(2,1)...) while((s32[]{:T(128)}, bf16[8,512,256]{2,1,0:T(8,128)(2,1)}, ...), condition=%wide.region_9.10_spmd, body=%wide.region_6.9_spmd.sunk | while | flops 555874304 | bytes 30475228 | solution.py:100
  657.8 18.8 all-gather
  678.7 19.8 all_gather.63
  707.9 45.2 %multiply_convert_fusion.2 = (bf16[2048,2048]{1,0:T(8,128)(2,1)}, f32[2048,2048]{1,0:T(8,128)}, f32[2048,2048]{1,0:T(8,128)}) fusion(f32[2048]{0:T(1024)S(1)} %bitcast.537, bf16[512,2048]{1,0:T(8,128)(2,1)} %all-gather.4.cloned.1.call-done, f32[2048,512]{1,0:T(8,128)} %copy-done.27, f32[512]{0:T(512)S(1)} %convert_element_type.423, ...), kind=kOutput, calls=%fused_computation.90 | convolution fusion | flops 4577034240 | bytes 48263168 | tf_op jit(solution)/shard_map/dot_general | solution.py:16
  773.7 22.8 fusion.78
  825.6 25.6 %all-to-all-done.8 = bf16[2,1024,512]{1,0,2:T(2,128)(2,1)} async-done(((bf16[2,1024,512]{1,0,2:T(2,128)(2,1)}), bf16[2,1024,512]{1,0,2:T(2,128)(2,1)}, u32[]{:S(2)}, u32[]{:S(2)}) %all-to-all-start.8) | async-done | bytes 2097184 | tf_op jit(solution)/shard_map/all_to_all | solution.py:342
  862.2 311.4 %while.117 = (s32[]{:T(128)}, bf16[2,2048,256]{2,1,0:T(8,128)(2,1)}, bf16[2,1024,256]{1,2,0:T(8,128)(2,1)}, bf16[2,1024,256]{1,2,0:T(8,128)(2,1)}, s32[2]{0:T(12...) while((s32[]{:T(128)}, bf16[2,2048,256]{2,1,0:T(8,128)(2,1)}, ...), condition=%wide.region_22.23_spmd, body=%wide.region_18.22_spmd.sunk | while | flops 1369438208 | bytes 130870040 | solution.py:183
  870.8 141.8 %while.121 = (s32[]{:T(128)}, f32[1024,4,64]{0,2,1:T(8,128)S(1)}, f32[1024,4,64]{0,2,1:T(8,128)}, bf16[4,512,256]{2,1,0:T(8,128)(2,1)}, s32[4]{0:T(128)S(1)}, /*...) while((s32[]{:T(128)}, f32[1024,4,64]{0,2,1:T(8,128)S(1)}, ...), condition=%wide.region_21.21_spmd.clone, body=%wide.region_19.20_spmd.clone.sunk | while | flops 1368913920 | bytes 117236624 | solution.py:174
  1026.5 141.8 %while.121 = (s32[]{:T(128)}, f32[1024,4,64]{0,2,1:T(8,128)S(1)}, f32[1024,4,64]{0,2,1:T(8,128)}, bf16[4,512,256]{2,1,0:T(8,128)(2,1)}, s32[4]{0:T(128)S(1)}, /*...) while((s32[]{:T(128)}, f32[1024,4,64]{0,2,1:T(8,128)S(1)}, ...), condition=%wide.region_21.21_spmd.clone, body=%wide.region_19.20_spmd.clone.sunk | while | flops 1368913920 | bytes 117236624 | solution.py:174
  1279.7 568.3 %while.120 = (s32[]{:T(128)}, bf16[2,2048,256]{2,1,0:T(8,128)(2,1)}, bf16[2,2048,256]{1,2,0:T(8,128)(2,1)}, bf16[2,2048,256]{1,2,0:T(8,128)(2,1)}, s32[2]{0:T(12...) while((s32[]{:T(128)}, bf16[2,2048,256]{2,1,0:T(8,128)(2,1)}, ...), condition=%wide.region_29.30_spmd.clone, body=%wide.region_25.29_spmd.clone.sunk | while | flops 2735471104 | bytes 247851760 | solution.py:183
  1288.6 269.6 %while.122 = (s32[]{:T(128)}, f32[2048,4,64]{0,2,1:T(8,128)}, f32[2048,4,64]{0,2,1:T(8,128)}, bf16[4,512,256]{2,1,0:T(8,128)(2,1)}, s32[4]{0:T(128)S(1)}, /*inde...) while((s32[]{:T(128)}, f32[2048,4,64]{0,2,1:T(8,128)}, ...), condition=%wide.region_28.28_spmd.clone, body=%wide.region_26.27_spmd.clone.sunk | while | flops 2734422528 | bytes 180700080 | solution.py:174
  1318.2 14.9 multiply_convert_fusion.5
  1384.7 14.9 multiply_convert_fusion.5
  1572.5 269.5 %while.122 = (s32[]{:T(128)}, f32[2048,4,64]{0,2,1:T(8,128)}, f32[2048,4,64]{0,2,1:T(8,128)}, bf16[4,512,256]{2,1,0:T(8,128)(2,1)}, s32[4]{0:T(128)S(1)}, /*inde...) while((s32[]{:T(128)}, f32[2048,4,64]{0,2,1:T(8,128)}, ...), condition=%wide.region_28.28_spmd.clone, body=%wide.region_26.27_spmd.clone.sunk | while | flops 2734422528 | bytes 180700080 | solution.py:174
  1602.1 14.9 multiply_convert_fusion.5
  1964.0 57.7 %all-reduce.15 = (bf16[512]{0:T(512)(128)(2,1)S(1)}, bf16[2048]{0:T(1024)(128)(2,1)S(1)}, bf16[512]{0:T(512)(128)(2,1)S(1)}, bf16[512]{0:T(512)(128)(2,1)S(1)}, ...) all-reduce(bf16[512]{0:T(512)(128)(2,1)S(1)} %dynamic-update-slice., ...), channel_id=1, replica_groups=mesh['fsdp'=16,'sp'=2] {'fsdp'}, use_global_device_ids=true, to_apply=%add.6 | all-reduce | flops 6144 | bytes 24576
  2045.4 16.5 reduce-scatter.31.cloned.1.call-done
  2063.4 56.9 %reduce-scatter.33.cloned.1.call-done = bf16[32,512]{1,0:T(8,128)(2,1)} async-done(((bf16[512,512]{1,0:T(8,128)(2,1)}), bf16[32,512]{1,0:T(8,128)(2,1)}) %reduce-scatter.33.cloned.1.call-update) | async-done | bytes 32784
  2121.9 57.1 %reduce-scatter.35.cloned.1.call-done = bf16[32,512]{1,0:T(8,128)(2,1)} async-done(((bf16[512,512]{1,0:T(8,128)(2,1)}), bf16[32,512]{1,0:T(8,128)(2,1)}) %reduce-scatter.35.cloned.1.call-update) | async-done | bytes 32784
  2180.5 56.9 %reduce-scatter.25.cloned.1.call-done = bf16[32,512]{1,0:T(8,128)(2,1)} async-done(((bf16[512,512]{1,0:T(8,128)(2,1)}), bf16[32,512]{1,0:T(8,128)(2,1)}) %reduce-scatter.25.cloned.1.call-update) | async-done | bytes 32784 | tf_op jit(solution)/shard_map/reduce_scatter | solution.py:408
  2237.4 58.6 %reduce-scatter.23.cloned.1.call-done = bf16[32,512]{1,0:T(8,128)(2,1)} async-done(((bf16[512,512]{1,0:T(8,128)(2,1)}), bf16[32,512]{1,0:T(8,128)(2,1)}) %reduce-scatter.23.cloned.1.call-update) | async-done | bytes 32784 | tf_op jit(solution)/shard_map/reduce_scatter | solution.py:399
  2296.0 58.4 %reduce-scatter.21.cloned.1.call-done = bf16[32,512]{1,0:T(8,128)(2,1)} async-done(((bf16[512,512]{1,0:T(8,128)(2,1)}), bf16[32,512]{1,0:T(8,128)(2,1)}) %reduce-scatter.21.cloned.1.call-update) | async-done | bytes 32784 | tf_op jit(solution)/shard_map/reduce_scatter | solution.py:396
  2360.5 33.8 %all-reduce.22.cloned.1.call-done = (bf16[32,512]{0,1:T(8,128)(2,1)}, bf16[32,512]{0,1:T(8,128)(2,1)}, bf16[32,512]{0,1:T(8,128)(2,1)}, bf16[32,512]{0,1:T(8,128...) async-done(((bf16[32,512]{0,1:T(8,128)(2,1)}, ...) | async-done | bytes 262864 | tf_op jit(solution)/shard_map/psum | solution.py:443
  (1043 shorter events, 1579.7 us)
Async XLA Ops:
  40.9 32.5 %all-to-all-start = ((bf16[2,1024,512]{1,0,2:T(2,128)(2,1)}), bf16[2,1024,512]{1,0,2:T(2,128)(2,1)}, u32[]{:S(2)}, u32[]{:S(2)}) async-start(bf16[2,1024,512]{1,0,2:T(2,128)(2,1)} %copy.93), calls=%async_computation | async-start | bytes 4194304 | tf_op jit(solution)/shard_map/all_to_all | solution.py:286
  73.4 35.7 %all-to-all-start.2 = ((bf16[2,1024,512]{1,0,2:T(2,128)(2,1)}), bf16[2,1024,512]{1,0,2:T(2,128)(2,1)}, u32[]{:S(2)}, u32[]{:S(2)}) async-start(bf16[2,1024,512]{1,0,2:T(2,128)(2,1)} %copy.97), calls=%async_computation.2 | async-start | bytes 4194304 | tf_op jit(solution)/shard_map/all_to_all | solution.py:285
  109.2 44.9 %all-to-all-start.1 = ((bf16[2,1024,512]{1,0,2:T(2,128)(2,1)}), bf16[2,1024,512]{1,0,2:T(2,128)(2,1)}, u32[]{:S(2)}, u32[]{:S(2)}) async-start(bf16[2,1024,512]{1,0,2:T(2,128)(2,1)} %copy.95), calls=%async_computation.1 | async-start | bytes 4194304 | tf_op jit(solution)/shard_map/all_to_all | solution.py:284
  362.1 110.7 %all-to-all-start.3 = ((bf16[2,2048,256]{2,0,1:T(2,128)(2,1)}), bf16[2,2048,256]{2,0,1:T(2,128)(2,1)}, u32[]{:S(2)}, u32[]{:S(2)}) async-start(bf16[2,2048,256]{2,0,1:T(2,128)(2,1)} %copy.100), calls=%async_computation.3 | async-start | bytes 4194304 | tf_op jit(solution)/shard_map/all_to_all | solution.py:289
  404.8 298.3 %copy-start.81 = (f32[512]{0:T(512)}, f32[512]{0:T(512)S(1)}, u32[]{:S(2)}) copy-start(f32[512]{0:T(512)S(1)} %convert_element_type.416) | copy-start | bytes 6148
  472.8 19.2 all-to-all-start.4
  492.0 17.5 all-to-all-start.6
  509.4 29.2 %all-to-all-start.5 = ((bf16[2,1024,512]{1,0,2:T(2,128)(2,1)}), bf16[2,1024,512]{1,0,2:T(2,128)(2,1)}, u32[]{:S(2)}, u32[]{:S(2)}) async-start(bf16[2,1024,512]{1,0,2:T(2,128)(2,1)} %copy.104), calls=%async_computation.5 | async-start | bytes 4194304 | tf_op jit(solution)/shard_map/all_to_all | solution.py:303
  514.2 193.7 %all-gather.4.cloned.1.call-start = ((), (), s32[]{:S(2)}) async-start(), calls=%async_computation.26 | async-start | bytes 2228224 | tf_op jit(solution)/shard_map/all_gather | solution.py:241
  652.0 46.6 %all-to-all-start.7 = ((bf16[2,2048,256]{2,0,1:T(2,128)(2,1)}), bf16[2,2048,256]{2,0,1:T(2,128)(2,1)}, u32[]{:S(2)}, u32[]{:S(2)}) async-start(bf16[2,2048,256]{2,0,1:T(2,128)(2,1)} %copy.109), calls=%async_computation.7 | async-start | bytes 4194304 | tf_op jit(solution)/shard_map/all_to_all | solution.py:308
  657.0 96.2 %all-gather.6.cloned.1.call-start = ((), (), s32[]{:S(2)}) async-start(), calls=%async_computation.27 | async-start | bytes 2228224 | tf_op jit(solution)/shard_map/all_gather | solution.py:243
  820.5 30.7 %all-to-all-start.8 = ((bf16[2,1024,512]{1,0,2:T(2,128)(2,1)}), bf16[2,1024,512]{1,0,2:T(2,128)(2,1)}, u32[]{:S(2)}, u32[]{:S(2)}) async-start(bf16[2,1024,512]{1,0,2:T(2,128)(2,1)} %copy.111), calls=%async_computation.8 | async-start | bytes 4194304 | tf_op jit(solution)/shard_map/all_to_all | solution.py:342
  1179.4 29.7 %all-to-all-start.9 = ((bf16[2,2048,256]{2,0,1:T(2,128)(2,1)}), bf16[2,2048,256]{2,0,1:T(2,128)(2,1)}, u32[]{:S(2)}, u32[]{:S(2)}) async-start(bf16[2,2048,256]{2,0,1:T(2,128)(2,1)} %copy.113), calls=%async_computation.9 | async-start | bytes 4194304 | tf_op jit(solution)/shard_map/all_to_all | solution.py:347
  1184.2 702.4 %reduce-scatter.27.cloned.1.call-start = ((), (), s32[]{:S(2)}) async-start(), calls=%async_computation.31 | async-start | bytes 2228224 | tf_op jit(solution)/shard_map/reduce_scatter | solution.py:411
  1209.1 26.0 %all-to-all-start.14 = ((bf16[2,1024,256]{2,0,1:T(2,128)(2,1)}), bf16[2,1024,256]{2,0,1:T(2,128)(2,1)S(1)}, u32[]{:S(2)}, u32[]{:S(2)}) async-start(bf16[2,1024,256]{2,0,1:T(2,128)(2,1)} %copy.125), calls=%async_computation.14 | async-start | bytes 2097152 | tf_op jit(solution)/shard_map/all_to_all | solution.py:348
  1235.1 29.0 %all-to-all-start.10 = ((bf16[2,1024,512]{1,0,2:T(2,128)(2,1)}), bf16[2,1024,512]{1,0,2:T(2,128)(2,1)}, u32[]{:S(2)}, u32[]{:S(2)}) async-start(bf16[2,1024,512]{1,0,2:T(2,128)(2,1)} %copy.115), calls=%async_computation.10 | async-start | bytes 4194304 | tf_op jit(solution)/shard_map/all_to_all | solution.py:369
  1240.1 646.5 %reduce-scatter.29.cloned.1.call-start = ((), (), s32[]{:S(2)}) async-start(), calls=%async_computation.32 | async-start | bytes 2228224 | tf_op jit(solution)/shard_map/reduce_scatter | solution.py:417
  1264.2 589.7 %all-to-all-start.15 = ((bf16[2,1024,256]{2,0,1:T(2,128)(2,1)}), bf16[2,1024,256]{2,0,1:T(2,128)(2,1)}, u32[]{:S(2)}, u32[]{:S(2)}) async-start(bf16[2,1024,256]{2,0,1:T(2,128)(2,1)} %copy.127), calls=%async_computation.15 | async-start | bytes 2097152 | tf_op jit(solution)/shard_map/all_to_all | solution.py:349
  1853.8 27.9 %all-to-all-start.11 = ((bf16[2,2048,256]{2,0,1:T(2,128)(2,1)}), bf16[2,2048,256]{2,0,1:T(2,128)(2,1)}, u32[]{:S(2)}, u32[]{:S(2)}) async-start(bf16[2,2048,256]{2,0,1:T(2,128)(2,1)} %copy.119), calls=%async_computation.11 | async-start | bytes 4194304 | tf_op jit(solution)/shard_map/all_to_all | solution.py:374
  1858.6 172.1 %reduce-scatter.37.cloned.1.call-start = ((), (), s32[]{:S(2)}) async-start(), calls=%async_computation.36 | async-start | bytes 557056
  1859.8 172.5 %reduce-scatter.39.cloned.1.call-start = ((), (), s32[]{:S(2)}) async-start(), calls=%async_computation.37 | async-start | bytes 557056
  1881.7 27.0 %all-to-all-start.12 = ((bf16[2,2048,256]{2,0,1:T(2,128)(2,1)}), bf16[2,2048,256]{2,0,1:T(2,128)(2,1)}, u32[]{:S(2)}, u32[]{:S(2)}) async-start(bf16[2,2048,256]{2,0,1:T(2,128)(2,1)} %copy.121), calls=%async_computation.12 | async-start | bytes 4194304 | tf_op jit(solution)/shard_map/all_to_all | solution.py:375
  1886.6 147.2 %all-reduce.24.cloned.1.call-start = ((), (), s32[]{:S(2)}) async-start(), calls=%async_computation.39 | async-start | bytes 524288 | tf_op jit(solution)/shard_map/psum | solution.py:451
  1887.3 174.6 %reduce-scatter.31.cloned.1.call-start = ((), (), s32[]{:S(2)}) async-start(), calls=%async_computation.33 | async-start | bytes 557056
  1908.7 26.1 %all-to-all-start.13 = ((bf16[2,2048,256]{2,0,1:T(2,128)(2,1)}), bf16[2,2048,256]{2,0,1:T(2,128)(2,1)}, u32[]{:S(2)}, u32[]{:S(2)}) async-start(bf16[2,2048,256]{2,0,1:T(2,128)(2,1)} %copy.123), calls=%async_computation.13 | async-start | bytes 4194304 | tf_op jit(solution)/shard_map/all_to_all | solution.py:376
  1913.6 206.8 %reduce-scatter.33.cloned.1.call-start = ((), (), s32[]{:S(2)}) async-start(), calls=%async_computation.34 | async-start | bytes 557056
  1921.5 257.4 %reduce-scatter.35.cloned.1.call-start = ((), (), s32[]{:S(2)}) async-start(), calls=%async_computation.35 | async-start | bytes 557056
  1942.7 294.7 %reduce-scatter.25.cloned.1.call-start = ((), (), s32[]{:S(2)}) async-start(), calls=%async_computation.30 | async-start | bytes 557056 | tf_op jit(solution)/shard_map/reduce_scatter | solution.py:408
  1951.3 344.7 %reduce-scatter.23.cloned.1.call-start = ((), (), s32[]{:S(2)}) async-start(), calls=%async_computation.29 | async-start | bytes 557056 | tf_op jit(solution)/shard_map/reduce_scatter | solution.py:399
  1959.0 395.4 %reduce-scatter.21.cloned.1.call-start = ((), (), s32[]{:S(2)}) async-start(), calls=%async_computation.28 | async-start | bytes 557056 | tf_op jit(solution)/shard_map/reduce_scatter | solution.py:396
  2029.9 364.4 %all-reduce.22.cloned.1.call-start = ((), (), s32[]{:S(2)}) async-start(), calls=%async_computation.38 | async-start | bytes 1515520 | tf_op jit(solution)/shard_map/psum | solution.py:443
  2042.1 312.3 %copy-start.40 = (bf16[512,512]{1,0:T(8,128)(2,1)S(1)}, bf16[512,512]{1,0:T(8,128)(2,1)}, u32[]{:S(2)}) copy-start(bf16[512,512]{1,0:T(8,128)(2,1)} %copy-done.39) | copy-start | bytes 1572868
  (174 other events, 2311.4 us)
Sparse Core Ops, SparseCore 0:
  517.2 40.2 all-gather.3
  660.0 41.5 all-gather.5
  1195.7 61.1 reduce-scatter.26
  1260.9 60.5 reduce-scatter.28
  1862.7 55.9 reduce-scatter.36
  1922.5 54.7 reduce-scatter.38
  1979.7 22.3 all-reduce.23
  2006.1 55.8 reduce-scatter.30
  2065.5 54.8 reduce-scatter.32
  2124.2 54.7 reduce-scatter.34
  2182.5 54.7 reduce-scatter.24
  2241.2 54.7 reduce-scatter.22
  2299.6 54.7 reduce-scatter.20
  2358.9 35.3 all-reduce.21
where the time goes:
time: 2440 us; the launch traced here: 2420 us
  matrix products  798 us (33%)
  local copies, waits for them, and re-layouts  475 us (19%)
  waiting for transfers between devices  435 us (18%)
  blocking collectives  273 us (11%)
  other arithmetic  272 us (11%)
  starting transfers between devices  76 us (3%)
  loops' own time  75.9 us (3%)
    dot_general x16, matrix products, one_one_block(): jnp.einsum('qhd,khd->hqk', query_part, key_part, preferred_element_type=j...  156 us
    convert_element_type x16, other arithmetic, one_one_block(): score_grad = (prob_rows * (prob_grad - row_inner)).astype(jnp.bfloat16)  135 us
    unnamed x19, waiting for transfers between devices  133 us
    dot_general x16, matrix products, one_one_block(): jnp.einsum('hqk,qhd->khd', prob_rows.astype(jnp.bfloat16), grad_part, pre...  123 us
    dot_general x16, matrix products, one_one_block(): jnp.einsum('qhd,khd->hqk', grad_part, value_part, preferred_element_type=...  115 us
    unnamed x2, blocking collectives  89.8 us
    dot_general x16, matrix products, one_one_block(): jnp.einsum('hqk,qhd->khd', score_grad, query_part, preferred_element_type...  80.8 us
    dot_general x10, matrix products, matmul(): return jnp.dot(left, right, preferred_element_type=jnp.float32)  76.2 us
  transfers between devices with their start and end apart: 30, of which 16 were waited for; matrix products, arithmetic and copies ran while one was open for 38% of the time, Pallas kernels for 0%

commit v1 on v0

v1 whole, which is shorter than its diff:
```python
import functools
import math

import jax
import jax.numpy as jnp
from jax import lax
from jax.experimental import pallas as pl
from jax.experimental.pallas import tpu as pltpu
from jax.sharding import PartitionSpec as P

HD = 64
BLK = 256
WINDOW = 4
EPS = 1e-05
MASKED = -1e30
LOG2E = 1.4426950408889634
LN2 = 0.6931471805599453
SAFE = 60.0
F32 = jnp.float32
BF16 = jnp.bfloat16
NN = (((1,), (0,)), ((), ()))
NT = (((1,), (1,)), ((), ()))
TN = (((0,), (0,)), ((), ()))
VMEM_LIMIT = 62 * 2**20


def dot(left, right, form=NN):
    return lax.dot_general(left, right, form, preferred_element_type=F32)


def norm(rows):
    center = rows - jnp.mean(rows, axis=0, keepdims=True)
    inverse = lax.rsqrt(jnp.mean(center * center, axis=0, keepdims=True) + EPS)
    return center * inverse, inverse


def norm_back(scaled, inverse, gain, upstream):
    through = upstream * gain
    return inverse * (
        through
        - jnp.mean(through, axis=0, keepdims=True)
        - scaled * jnp.mean(through * scaled, axis=0, keepdims=True)
    )


def fold(values):
    total = values[:, :128]
    for start in range(128, values.shape[1], 128):
        total = total + values[:, start : start + 128]
    return total


def gelu_pair(x):
    size = jnp.abs(x)
    t = 1.0 / (1.0 + (0.3275911 / math.sqrt(2.0)) * size)
    bell = jnp.exp2((-0.5 * LOG2E) * (x * x))
    series = t * (
        0.127414796 + t * (-0.142248368 + t * (0.7107068705 + t * (-0.7265760135 + t * 0.5307027145)))
    )
    tail = series * bell
    phi = jnp.where(x >= 0.0, 1.0 - tail, tail)
    return x * phi, phi + x * bell * (1.0 / math.sqrt(2.0 * math.pi))


def weight(pack, first, rows):
    return jnp.concatenate([pack[f, first : first + rows, :] for f in range(pack.shape[0])], axis=0)


def unpack_weight(pack, first, rows, plain=None, turned=None):
    whole = weight(pack, first, rows)
    if plain is not None:
        plain[...] = whole
    if turned is not None:
        turned[...] = whole.T


def attend(count, exact, keys, values, off, query, probs, mixed, inverse, bias):
    head_count = query.shape[0] // HD

    def scores(hs, j):
        part = dot(keys[hs, pl.ds(off + j * BLK, BLK)], query[hs, :], TN)
        if bias is not None:
            part = part + bias[j * BLK : (j + 1) * BLK, :]
        return part

    def first(h, hs):
        total = None
        if exact:
            parts = [scores(hs, j) for j in range(count)]
            top = jnp.max(parts[0], axis=0, keepdims=True)
            for part in parts[1:]:
                top = jnp.maximum(top, jnp.max(part, axis=0, keepdims=True))
        for j in range(count):
            terms = jnp.exp2(parts[j] - top if exact else scores(hs, j))
            partial = jnp.sum(terms.reshape(BLK // 8, 8, BLK), axis=0)
            total = partial if total is None else total + partial
            probs[h, j * BLK : (j + 1) * BLK, :] = terms.astype(BF16)
        return total

    def second(h, hs, total):
        sums = dot(values[hs, pl.ds(off, count * BLK)], probs[h, : count * BLK, :])
        scale = 1.0 / jnp.sum(total, axis=0, keepdims=True)
        mixed[hs, :] = (sums * scale).astype(BF16)
        inverse[pl.ds(h, 1), :] = scale

    if exact:

        def one(h, carry):
            hs = pl.ds(pl.multiple_of(h * HD, HD), HD)
            second(h, hs, first(h, hs))
            return carry

        lax.fori_loop(0, head_count, one, 0)
        return
    waiting = None
    for h in range(head_count):
        total = first(h, slice(h * HD, (h + 1) * HD))
        if h > 0:
            second(h - 1, slice((h - 1) * HD, h * HD), waiting)
        waiting = total
    second(head_count - 1, slice((head_count - 1) * HD, head_count * HD), waiting)


def attend_back(
    count, keys, values, off, query, grad, inner, probs, kept, query_grad, key_grad, value_grad
):
    head_count = query.shape[0] // HD

    def first(h):
        hs = slice(h * HD, (h + 1) * HD)
        for j in range(count):
            us = slice(j * BLK, (j + 1) * BLK)
            prob_grad = dot(values[hs, pl.ds(off + j * BLK, BLK)], grad[hs, :], TN)
            kept[h, us, :] = (probs[h, us, :].astype(F32) * (prob_grad - inner[h : h + 1, :])).astype(BF16)

    def second(h):
        hs = slice(h * HD, (h + 1) * HD)
        us = slice(0, count * BLK)
        window = pl.ds(off, count * BLK)
        query_grad[hs, :] = (dot(keys[hs, window], kept[h, us, :]) * (1.0 / math.sqrt(HD))).astype(BF16)
        key_grad[hs, window] += dot(query[hs, :], kept[h, us, :], NT)
        value_grad[hs, window] += dot(grad[hs, :], probs[h, us, :], NT)

    first(0)
    for h in range(1, head_count):
        first(h)
        second(h - 1)
    second(head_count - 1)


def scale_grad(mixed_grad, mixed, inverse, grad, inner):
    for h in range(mixed.shape[0] // HD):
        hs = slice(h * HD, (h + 1) * HD)
        scaled = mixed_grad[hs, :] * inverse[h : h + 1, :]
        grad[hs, :] = scaled.astype(BF16)
        inner[h : h + 1, :] = jnp.sum(scaled * mixed[hs, :].astype(F32), axis=0, keepdims=True)


def head_norms(rows, head_count):
    found = []
    for h in range(head_count):
        part = rows[h * HD : (h + 1) * HD, :].astype(F32)
        found.append(jnp.max(jnp.sum(part * part, axis=0, keepdims=True), axis=1, keepdims=True))
    return found


def safe_scores(query, key_norms):
    head_count = query.shape[0] // HD
    worst = None
    for h, found in enumerate(head_norms(query[...], head_count)):
        product = found * key_norms[h : h + 1, 0:1]
        worst = product if worst is None else jnp.maximum(worst, product)
    return jnp.max(worst) < SAFE * SAFE


def store_key_norms(key_norms, keys):
    head_count = keys.shape[0] // HD
    for h, found in enumerate(head_norms(keys[...], head_count)):
        key_norms[h : h + 1, :] = jnp.broadcast_to(found, (1, key_norms.shape[1]))


def doc_span(docs, seq, block, block_count):
    mine = docs[seq, block]
    low = jnp.int32(0)
    count = jnp.int32(0)
    for b in range(block_count):
        low = low + jnp.where(docs[seq, b] < mine, 1, 0).astype(jnp.int32)
        count = count + jnp.where(docs[seq, b] == mine, 1, 0).astype(jnp.int32)
    return low, count


def self_forward_kernel(
    shard, docs, place, hidden, own_tokens, far_tokens, order, reach, pack, cols,
    keys, values, query, mixed, probs, inverse, scaled1, inverse1,
    q_turned, k_turned, v_turned, o_turned, bias, key_norms,
):
    seq, step = pl.program_id(0), pl.program_id(1)
    steps = pl.num_programs(1)
    rows = shard
    local = own_tokens.shape[1]
    parts = far_tokens.shape[0] + 1
    block_count = order.shape[1]
    me = place[0]

    @pl.when((seq == 0) & (step == 0))
    def _():
        for which, turned in enumerate((q_turned, k_turned, v_turned, o_turned)):
            unpack_weight(pack, which * rows, rows, None, turned)

    @pl.when(step == 0)
    def _():
        for part in range(parts):
            tokens = own_tokens[0] if part == 0 else far_tokens[part - 1, 0]
            owner = lax.rem(me + part, parts)
            at = pl.ds(pl.multiple_of(owner * local, BLK), local)
            turned = tokens.T
            keys[0, :, at] = dot(k_turned[...], turned).astype(BF16)
            values[0, :, at] = dot(v_turned[...], turned).astype(BF16)
        store_key_norms(key_norms, keys.at[0])

    block = me * steps + step
    low, count = doc_span(docs, seq, block, block_count)
    turned = hidden[0].T
    query[0] = (dot(q_turned[...], turned) * (LOG2E / math.sqrt(HD))).astype(BF16)

    order_turned = order[0].astype(F32).T
    lanes = lax.broadcasted_iota(jnp.int32, order_turned.shape, 1)
    reach_row = reach[0, pl.ds(block, 1), :].astype(F32)
    differ = lax.broadcasted_iota(jnp.int32, (BLK, BLK), 0) != lax.broadcasted_iota(
        jnp.int32, (BLK, BLK), 1
    )
    for j in range(WINDOW):
        at = low + j
        column = jnp.sum(jnp.where(lanes == at, order_turned, 0.0), axis=1, keepdims=True)
        seen = (column < reach_row) & (differ | (at != block))
        bias[j * BLK : (j + 1) * BLK, :] = jnp.where(seen, 0.0, MASKED)

    safe = safe_scores(query.at[0], key_norms)
    off = pl.multiple_of(low * BLK, BLK)
    for size in range(1, WINDOW + 1):
        for exact in (False, True):

            @pl.when((count == size) & (safe != exact))
            def _(size=size, exact=exact):
                attend(
                    size, exact, keys.at[0], values.at[0], off, query.at[0], probs.at[0, 0],
                    mixed.at[0], inverse.at[0, 0], bias,
                )

    first_sum = turned.astype(F32) + dot(o_turned[...], mixed[0])
    center, inv = norm(first_sum)
    scaled1[0] = center
    inverse1[0, 0] = jnp.broadcast_to(inv, inverse1.shape[2:])


def cross_ffn_kernel(
    shard, inner_shard, scaled1, own_enc, far_enc, out_grad, pack, big_pack, cols, inner_bias,
    keys, values, query, mixed, probs, inverse, second_grad, layer_out, inner_out, outer_out, col_grads,
    bias_grad,
    q_turned, k_turned, v_turned, o_turned, inner, inner_turned, outer, outer_turned, inner_acc, outer_acc,
    sums, bias_sum, key_norms, slope,
):
    seq, step = pl.program_id(0), pl.program_id(1)
    rows = shard
    first_step = (seq == 0) & (step == 0)
    last_step = (seq == pl.num_programs(0) - 1) & (step == pl.num_programs(1) - 1)
    local = own_enc.shape[1]
    parts = far_enc.shape[0] + 1
    width = inner.shape[0]
    owners = pack.shape[0]
    chunks = inner.shape[1] // width
    outer_rows = outer.shape[0] // owners

    @pl.when(first_step)
    def _():
        for which, turned in enumerate((q_turned, k_turned, v_turned, o_turned)):
            unpack_weight(pack, which * rows, rows, None, turned)
        for c in range(chunks):
            cs = slice(c * width, (c + 1) * width)
            whole = weight(big_pack, c * rows, rows)
            inner[:, cs] = whole
            inner_turned[cs, :] = whole.T
        for f in range(owners):
            fs = slice(f * outer_rows, (f + 1) * outer_rows)
            outer[fs, :] = big_pack[f, chunks * rows : chunks * rows + outer_rows, :]
        for c in range(chunks):
            cs = slice(c * width, (c + 1) * width)
            outer_turned[:, cs] = outer[cs, :].T
        inner_acc[...] = jnp.zeros_like(inner_acc)
        outer_acc[...] = jnp.zeros_like(outer_acc)
        sums[...] = jnp.zeros_like(sums)
        bias_sum[...] = jnp.zeros_like(bias_sum)

    @pl.when(step == 0)
    def _():
        for part in range(parts):
            turned = (own_enc[0] if part == 0 else far_enc[part - 1, 0]).T
            at = slice(part * local, (part + 1) * local)
            keys[0, :, at] = dot(k_turned[...], turned).astype(BF16)
            values[0, :, at] = dot(v_turned[...], turned).astype(BF16)
        store_key_norms(key_norms, keys.at[0])

    normed = scaled1[0] * cols[:, 0:1] + cols[:, 1:2]
    query[0] = (dot(q_turned[...], normed.astype(BF16)) * (LOG2E / math.sqrt(HD))).astype(BF16)
    safe = safe_scores(query.at[0], key_norms)
    for exact in (False, True):

        @pl.when(safe != exact)
        def _(exact=exact):
            attend(
                parts * local // BLK, exact, keys.at[0], values.at[0], 0, query.at[0], probs.at[0, 0],
                mixed.at[0], inverse.at[0, 0], None,
            )

    second_sum = normed + dot(o_turned[...], mixed[0])
    scaled2, inverse2 = norm(second_sum)
    gain2 = cols[:, 2:3]
    middle = scaled2 * gain2 + cols[:, 3:4]
    middle_low = middle.astype(BF16)
    pre = dot(inner_turned[...], middle_low) + inner_bias[...]
    active, pull = gelu_pair(pre)
    active = active.astype(BF16)
    slope[...] = pull.astype(BF16)
    third_sum = middle + dot(outer_turned[...], active) + cols[:, 6:7]
    scaled3, inverse3 = norm(third_sum)
    gain3 = cols[:, 4:5]
    layer_out[0] = (scaled3 * gain3 + cols[:, 5:6]).T
    upstream = out_grad[0].T.astype(F32)
    third_grad = norm_back(scaled3, inverse3, gain3, upstream)
    sums[2] += fold(upstream * scaled3)
    sums[3] += fold(upstream)
    outer_low = third_grad.astype(BF16)
    sums[4] += fold(outer_low.astype(F32))
    outer_acc[...] += dot(active, outer_low, NT)
    inner_low = (dot(outer[...], outer_low) * slope[...].astype(F32)).astype(BF16)
    bias_sum[...] += fold(inner_low.astype(F32))
    inner_acc[...] += dot(middle_low, inner_low, NT)
    middle_grad = third_grad + dot(inner[...], inner_low)
    sums[0] += fold(middle_grad * scaled2)
    sums[1] += fold(middle_grad)
    second_grad[0] = norm_back(scaled2, inverse2, gain2, middle_grad)

    @pl.when(last_step)
    def _():
        for f in range(owners):
            for c in range(chunks):
                inner_out[f, c * rows : (c + 1) * rows, :] = inner_acc[
                    f * rows : (f + 1) * rows, c * width : (c + 1) * width
                ].astype(BF16)
            outer_out[f] = outer_acc[f * outer_rows : (f + 1) * outer_rows, :].astype(BF16)
        for which in range(5):
            col_grads[:, which : which + 1] = jnp.sum(sums[which], axis=1, keepdims=True)
        bias_grad[...] = jnp.sum(bias_sum[...], axis=1, keepdims=True)


def pack_grad(out, first, rows, acc):
    for f in range(out.shape[0]):
        out[f, first : first + rows, :] = acc[f * rows : (f + 1) * rows, :].astype(BF16)


def cross_back_kernel(
    shard, second_grad, scaled1, inverse1, own_enc, far_enc, keys, values, query, mixed, probs, inverse,
    self_mixed, pack, self_pack, cols,
    first_grad, self_mixed_grad, own_part, far_part, grads, col_grads,
    q_plain, k_plain, v_plain, o_plain, so_plain, accs, sums, key_acc, value_acc, kept, grad, inner, query_grad,
):
    seq, step = pl.program_id(0), pl.program_id(1)
    rows = shard
    first_step = (seq == 0) & (step == 0)
    last_step = (seq == pl.num_programs(0) - 1) & (step == pl.num_programs(1) - 1)
    local = own_enc.shape[1]
    parts = far_enc.shape[0] + 1

    @pl.when(first_step)
    def _():
        for which, plain in enumerate((q_plain, k_plain, v_plain, o_plain)):
            unpack_weight(pack, which * rows, rows, plain, None)
        unpack_weight(self_pack, 3 * rows, rows, so_plain, None)
        accs[...] = jnp.zeros_like(accs)
        sums[...] = jnp.zeros_like(sums)

    @pl.when(step == 0)
    def _():
        key_acc[...] = jnp.zeros_like(key_acc)
        value_acc[...] = jnp.zeros_like(value_acc)

    cross_low = second_grad[0].astype(BF16)
    scale_grad(dot(o_plain[...], cross_low), mixed.at[0], inverse.at[0, 0], grad, inner)
    accs[3] += dot(mixed[0], cross_low, NT)
    attend_back(
        parts * local // BLK, keys.at[0], values.at[0], 0, query.at[0], grad, inner, probs.at[0, 0],
        kept, query_grad, key_acc, value_acc,
    )
    scaled = scaled1[0]
    gain = cols[:, 0:1]
    normed_low = (scaled * gain + cols[:, 1:2]).astype(BF16)
    accs[0] += dot(normed_low, query_grad[...], NT)
    normed_grad = second_grad[0] + dot(q_plain[...], query_grad[...])
    sums[0] += fold(normed_grad * scaled)
    sums[1] += fold(normed_grad)
    through = norm_back(scaled, inverse1[0, 0, 0:1, :], gain, normed_grad)
    first_grad[0] = through
    self_low = through.astype(BF16)
    accs[4] += dot(self_mixed[0], self_low, NT)
    self_mixed_grad[0] = dot(so_plain[...], self_low).astype(BF16)

    @pl.when(step == pl.num_programs(1) - 1)
    def _():
        for part in range(parts):
            at = slice(part * local, (part + 1) * local)
            key_low = (key_acc[:, at] * LN2).astype(BF16)
            value_low = value_acc[:, at].astype(BF16)
            turned = (own_enc[0] if part == 0 else far_enc[part - 1, 0]).T
            accs[1] += dot(turned, key_low, NT)
            accs[2] += dot(turned, value_low, NT)
            whole = (dot(k_plain[...], key_low) + dot(v_plain[...], value_low)).T
            if part == 0:
                own_part[0] = whole
            else:
                far_part[part - 1, 0] = whole.astype(BF16)

    @pl.when(last_step)
    def _():
        for which in range(5):
            pack_grad(grads, which * rows, rows, accs.at[which])
        for which in range(2):
            col_grads[:, which : which + 1] = jnp.sum(sums[which], axis=1, keepdims=True)


def self_back_kernel(
    shard, docs, place, hidden, first_grad, own_tokens, far_tokens, keys, values, query, mixed, probs, inverse,
    mixed_grad, pack,
    hidden_grad, own_part, far_part, grads,
    q_plain, k_plain, v_plain, accs, key_acc, value_acc, kept, grad, inner, query_grad,
):
    seq, step = pl.program_id(0), pl.program_id(1)
    steps = pl.num_programs(1)
    rows = shard
    first_step = (seq == 0) & (step == 0)
    last_step = (seq == pl.num_programs(0) - 1) & (step == steps - 1)
    local = own_tokens.shape[1]
    parts = far_tokens.shape[0] + 1
    me = place[0]
    block_count = parts * steps

    @pl.when(first_step)
    def _():
        for which, plain in enumerate((q_plain, k_plain, v_plain)):
            unpack_weight(pack, which * rows, rows, plain, None)
        accs[...] = jnp.zeros_like(accs)

    @pl.when(step == 0)
    def _():
        key_acc[...] = jnp.zeros_like(key_acc)
        value_acc[...] = jnp.zeros_like(value_acc)

    low, count = doc_span(docs, seq, me * steps + step, block_count)
    off = pl.multiple_of(low * BLK, BLK)
    scale_grad(mixed_grad[0].astype(F32), mixed.at[0], inverse.at[0, 0], grad, inner)
    for size in range(1, WINDOW + 1):

        @pl.when(count == size)
        def _(size=size):
            attend_back(
                size, keys.at[0], values.at[0], off, query.at[0], grad, inner, probs.at[0, 0],
                kept, query_grad, key_acc, value_acc,
            )

    accs[0] += dot(hidden[0].T, query_grad[...], NT)
    hidden_grad[0] = (first_grad[0] + dot(q_plain[...], query_grad[...])).T

    @pl.when(step == steps - 1)
    def _():
        for part in range(parts):
            owner = lax.rem(me + part, parts)
            at = pl.ds(pl.multiple_of(owner * local, BLK), local)
            key_low = (key_acc[:, at] * LN2).astype(BF16)
            value_low = value_acc[:, at].astype(BF16)
            turned = (own_tokens[0] if part == 0 else far_tokens[part - 1, 0]).T
            accs[1] += dot(turned, key_low, NT)
            accs[2] += dot(turned, value_low, NT)
            whole = (dot(k_plain[...], key_low) + dot(v_plain[...], value_low)).T
            if part == 0:
                own_part[0] = whole
            else:
                far_part[part - 1, 0] = whole.astype(BF16)

    @pl.when(last_step)
    def _():
        for which in range(3):
            pack_grad(grads, which * rows, rows, accs.at[which])


def whole_spec():
    return pl.BlockSpec(memory_space=pltpu.VMEM)


def call(body, grid, scalars, in_specs, out_specs, out_shape, scratch, flops, args):
    return pl.pallas_call(
        body,
        grid_spec=pltpu.PrefetchScalarGridSpec(
            num_scalar_prefetch=scalars,
            grid=grid,
            in_specs=in_specs,
            out_specs=out_specs,
            scratch_shapes=scratch,
        ),
        out_shape=[jax.ShapeDtypeStruct(shape, kind) for shape, kind in out_shape],
        compiler_params=pltpu.CompilerParams(vmem_limit_bytes=VMEM_LIMIT),
        cost_estimate=pl.CostEstimate(flops=flops, bytes_accessed=2**25, transcendentals=0),
    )(*args)


def shift(array, axis, by, size):
    return lax.ppermute(array, axis, [((i + by) % size, i) for i in range(size)])


def others(array, size):
    return jnp.stack([shift(array, "sp", r, size) for r in range(1, size)])


def gather(parts):
    packed = jnp.concatenate(parts, axis=0)
    return lax.all_gather(packed, "fsdp", axis=0, tiled=False)


def on_device(sp, fsdp, *arrays):
    (
        hidden_in, token_stream, encoder_out, out_grad, doc_ids, key_order, context_size,
        self_query, self_key, self_value, self_output, cross_query, cross_key, cross_value, cross_output,
        inner_weight, inner_bias, outer_weight, outer_bias, first_gain, first_shift, second_gain,
        second_shift, third_gain, third_shift,
    ) = arrays
    seqs, local, width = hidden_in.shape
    enc_local = encoder_out.shape[1]
    shard, hidden_width = inner_weight.shape
    outer_rows = outer_weight.shape[0]
    chunks = hidden_width // width
    steps = local // BLK
    heads = width // HD
    length = local * sp
    enc_len = enc_local * sp
    block_count = key_order.shape[1]

    vectors = (inner_bias, first_gain, first_shift, second_gain, second_shift, third_gain, third_shift, outer_bias)
    flat = jnp.concatenate(vectors)
    tray = 16
    flat = jnp.pad(flat, (0, tray * width - flat.shape[0])).reshape(tray, width)
    self_pack = gather((self_query, self_key, self_value, self_output, flat))
    cross_pack = gather((cross_query, cross_key, cross_value, cross_output))
    big_pack = gather(tuple(jnp.split(inner_weight, chunks, axis=1)) + (outer_weight,))
    spread = self_pack[:, 4 * shard, :].astype(F32)
    bias_rows = inner_bias.shape[0]
    inner_bias_col = spread[:, :bias_rows].reshape(-1, 1)
    cols = (
        spread[:, bias_rows : bias_rows + 7 * shard]
        .reshape(fsdp, 7, shard)
        .transpose(0, 2, 1)
        .reshape(width, 7)
    )
    cols = jnp.pad(cols, ((0, 0), (0, 1)))

    far_tokens = others(token_stream, sp)
    far_enc = others(encoder_out, sp)
    place = lax.axis_index("sp").astype(jnp.int32).reshape(1)

    grid = (seqs, steps)
    whole = whole_spec()
    turned_spec = pl.BlockSpec((1, width, BLK), lambda s, i, *_: (s, 0, i))
    plain_spec = pl.BlockSpec((1, BLK, width), lambda s, i, *_: (s, i, 0))
    per_seq = lambda shape: pl.BlockSpec((1,) + shape, lambda s, i, *_: (s, 0, 0))
    far_seq = lambda rows: pl.BlockSpec((sp - 1, 1, rows, width), lambda s, i, *_: (0, s, 0, 0))
    rows_spec = pl.BlockSpec((1, 1, 8, BLK), lambda s, i, *_: (s, i, 0, 0))
    probs_spec = lambda keys: pl.BlockSpec((1, 1, heads, keys, BLK), lambda s, i, *_: (s, i, 0, 0, 0))
    turned_shape = (seqs, width, local)
    rows_shape = (seqs, steps, 8, BLK)
    square = pltpu.VMEM((width, width), BF16)
    rows_count = seqs * local
    window = WINDOW * BLK

    keys, values, query, mixed, probs, inverse, scaled1, inverse1 = call(
        functools.partial(self_forward_kernel, shard),
        grid, 2,
        [
            plain_spec, per_seq((local, width)), far_seq(local), per_seq((block_count, BLK)),
            per_seq((block_count, BLK)), whole, whole,
        ],
        [
            per_seq((width, length)), per_seq((width, length)), turned_spec, turned_spec, probs_spec(window),
            rows_spec, turned_spec, rows_spec,
        ],
        [
            ((seqs, width, length), BF16), ((seqs, width, length), BF16), (turned_shape, BF16),
            (turned_shape, BF16), ((seqs, steps, heads, window, BLK), BF16), (rows_shape, F32),
            (turned_shape, F32), (rows_shape, F32),
        ],
        [square] * 4 + [pltpu.VMEM((window, BLK), F32), pltpu.VMEM((heads, 128), F32)],
        rows_count * width * width * 12,
        (doc_ids, place, hidden_in, token_stream, far_tokens, key_order, context_size, self_pack, cols),
    )

    big = lambda a, b, kind: pltpu.VMEM((a, b), kind)
    (
        cross_keys, cross_values, cross_q, cross_mixed, cross_probs, cross_inverse, second_grad, layer_out,
        inner_grad, outer_grad, late_cols, bias_grad,
    ) = call(
        functools.partial(cross_ffn_kernel, shard, 0),
        grid, 0,
        [
            turned_spec, per_seq((enc_local, width)), far_seq(enc_local), plain_spec, whole, whole, whole, whole,
        ],
        [
            per_seq((width, enc_len)), per_seq((width, enc_len)), turned_spec, turned_spec, probs_spec(enc_len),
            rows_spec, turned_spec, plain_spec, whole, whole, whole, whole,
        ],
        [
            ((seqs, width, enc_len), BF16), ((seqs, width, enc_len), BF16), (turned_shape, BF16),
            (turned_shape, BF16), ((seqs, steps, heads, enc_len, BLK), BF16), (rows_shape, F32),
            (turned_shape, F32), ((seqs, local, width), F32), ((fsdp, chunks * shard, width), BF16),
            ((fsdp, outer_rows, width), BF16), ((width, 8), F32), ((hidden_width, 1), F32),
        ],
        [square] * 4
        + [
            big(width, hidden_width, BF16), big(hidden_width, width, BF16), big(hidden_width, width, BF16),
            big(width, hidden_width, BF16), big(width, hidden_width, F32), big(hidden_width, width, F32),
            pltpu.VMEM((5, width, 128), F32), big(hidden_width, 128, F32), big(heads, 128, F32),
            big(hidden_width, BLK, BF16),
        ],
        rows_count * width * width * 60,
        (scaled1, encoder_out, far_enc, out_grad, cross_pack, big_pack, cols, inner_bias_col),
    )

    attention_scratch = lambda keys_len, kept_len: [
        big(width, keys_len, F32), big(width, keys_len, F32), pltpu.VMEM((heads, kept_len, BLK), BF16),
        big(width, BLK, BF16), big(heads, BLK, F32), big(width, BLK, BF16),
    ]
    first_grad, mixed_grad, own_enc_part, far_enc_part, cross_grads, early_cols = call(
        functools.partial(cross_back_kernel, shard),
        grid, 0,
        [
            turned_spec, turned_spec, rows_spec, per_seq((enc_local, width)), far_seq(enc_local),
            per_seq((width, enc_len)), per_seq((width, enc_len)), turned_spec, turned_spec, probs_spec(enc_len),
            rows_spec, turned_spec, whole, whole, whole,
        ],
        [
            turned_spec, turned_spec, per_seq((enc_local, width)), far_seq(enc_local), whole, whole,
        ],
        [
            (turned_shape, F32), (turned_shape, BF16), ((seqs, enc_local, width), F32),
            ((sp - 1, seqs, enc_local, width), BF16), ((fsdp, 5 * shard, width), BF16), ((width, 8), F32),
        ],
        [square] * 5
        + [pltpu.VMEM((5, width, width), F32), pltpu.VMEM((2, width, 128), F32)]
        + attention_scratch(enc_len, enc_len),
        rows_count * width * width * 30,
        (
            second_grad, scaled1, inverse1, encoder_out, far_enc, cross_keys, cross_values, cross_q, cross_mixed,
            cross_probs, cross_inverse, mixed, cross_pack, self_pack, cols,
        ),
    )

    hidden_grad, own_part, far_part, self_grads = call(
        functools.partial(self_back_kernel, shard),
        grid, 2,
        [
            plain_spec, turned_spec, per_seq((local, width)), far_seq(local), per_seq((width, length)),
            per_seq((width, length)), turned_spec, turned_spec, probs_spec(window), rows_spec, turned_spec, whole,
        ],
        [plain_spec, per_seq((local, width)), far_seq(local), whole],
        [
            ((seqs, local, width), F32), ((seqs, local, width), F32), ((sp - 1, seqs, local, width), BF16),
            ((fsdp, 3 * shard, width), BF16),
        ],
        [square] * 3 + [pltpu.VMEM((3, width, width), F32)] + attention_scratch(length, window),
        rows_count * width * width * 30,
        (
            doc_ids, place, hidden_in, first_grad, token_stream, far_tokens, keys, values, query, mixed, probs,
            inverse, mixed_grad, self_pack,
        ),
    )

    def settle(own, far):
        for r in range(1, sp):
            own = own + shift(far[r - 1], "sp", -r, sp).astype(F32)
        return own

    token_grad = settle(own_part, far_part)
    encoder_grad = settle(own_enc_part, far_enc_part)

    def reduce(grads):
        mine = lax.psum_scatter(grads, "fsdp", scatter_dimension=0, tiled=True)[0]
        total = mine.astype(F32)
        for r in range(1, sp):
            total = total + shift(mine, "sp", r, sp).astype(F32)
        return total

    inner_total = reduce(inner_grad)
    inner_total = jnp.concatenate([inner_total[c * shard : (c + 1) * shard] for c in range(chunks)], axis=1)
    outer_total = reduce(outer_grad)
    cross_total = reduce(cross_grads)
    col_grads = jnp.concatenate([early_cols[:, :2], late_cols[:, :5]], axis=1)
    small = jnp.concatenate(
        [
            bias_grad.reshape(fsdp, bias_rows),
            col_grads.reshape(fsdp, shard, 7).transpose(0, 2, 1).reshape(fsdp, 7 * shard),
        ],
        axis=1,
    ).astype(BF16)
    small = jnp.pad(small, ((0, 0), (0, tray * width - small.shape[1]))).reshape(fsdp, tray, width)
    self_total = reduce(jnp.concatenate([self_grads, small], axis=1))
    flat = self_total[3 * shard :].reshape(-1)
    cut = lambda total, k: total[k * shard : (k + 1) * shard]
    vec = lambda k: flat[bias_rows + k * shard : bias_rows + (k + 1) * shard]
    return (
        layer_out, hidden_grad, token_grad, encoder_grad,
        cut(self_total, 0), cut(self_total, 1), cut(self_total, 2), cut(cross_total, 4),
        cut(cross_total, 0), cut(cross_total, 1), cut(cross_total, 2), cut(cross_total, 3),
        inner_total, flat[:bias_rows], outer_total, vec(6), vec(0), vec(1), vec(2), vec(3), vec(4), vec(5),
    )


def solution(mesh):
    tokens, table, vector = P("fsdp", "sp", None), P("fsdp", None), P("fsdp")
    order = P("fsdp", None, None)
    return jax.shard_map(
        functools.partial(on_device, mesh.shape["sp"], mesh.shape["fsdp"]),
        mesh=mesh,
        in_specs=(tokens,) * 4
        + (table, order, order)
        + (table,) * 9
        + (vector, table)
        + (vector,) * 7,
        out_specs=(tokens,) * 4 + (table,) * 9 + (vector, table) + (vector,) * 7,
        check_vma=False,
    )
```

time: 2440 us -> 688 us (0.28)
  matrix products: 798 us -> 0 us
  local copies, waits for them, and re-layouts: 475 us -> 21.2 us
  blocking collectives: 273 us -> 0 us
  Pallas kernels: 0 us -> 272 us
  other arithmetic: 272 us -> 19.3 us
  waiting for transfers between devices: 435 us -> 341 us
  loops' own time: 75.9 us -> 0 us
  starting transfers between devices: 76 us -> 11.8 us
    dot_general x142 -> x0, matrix products: 798 us -> none  [the longest x16 156 us: one_one_block(): jnp.einsum('qhd,khd->hqk', query_part, key_part, preferred_element_type=j...]
    pallas_call x0 -> x4, Pallas kernels: none -> 272 us  [call(): pl.pallas_call(body, grid_spec=pltpu.PrefetchScalarGridSpec(num_scalar_pr...]
    all_gather x9 -> x0, blocking collectives: 183 us -> none  [the longest x1 24.9 us: on_device(): lax.all_gather(self_value, 'fsdp', axis=0, tiled=True)]
    convert_element_type x46 -> x1, other arithmetic: 162 us -> 0.92 us  [on_device(): spread = self_pack[:, 4 * shard, :].astype(F32)]
    unnamed x19 -> x7, waiting for transfers between devices: 133 us -> 1.13 us
    dynamic_slice x130 -> x0, local copies, waits for them, and re-layouts: 120 us -> none  [the longest x16 31.9 us: attend_one_block(): lax.dynamic_index_in_dim(key_rows, seq_index, 0, False)]
    all_to_all x16 -> x0, waiting for transfers between devices: 94.8 us -> none  [the longest x1 25.6 us: on_device(): lax.all_to_all(cross_mixed, 'sp', split_axis=2, concat_axis=1, tiled=True)]
    all_to_all x24 -> x0, local copies, waits for them, and re-layouts: 94.7 us -> none  [the longest x2 9.62 us: on_device(): lax.all_to_all(self_mixed, 'sp', split_axis=2, concat_axis=1, tiled=True)]
  transfers between devices with their start and end apart: 30 -> 15, of which waited for: 16 -> 10; matrix products, arithmetic and copies ran while one was open for 38% -> 3% of each run, Pallas kernels for 0% -> 9%
where the time goes in v1:
time: 688 us; the launch traced here: 680 us
  waiting for transfers between devices  341 us (50%)
  Pallas kernels  272 us (40%)
  local copies, waits for them, and re-layouts  21.2 us (3%)
  other arithmetic  19.3 us (3%)
  between operations  14.5 us (2%)
  starting transfers between devices  11.8 us (2%)
    pallas_call x4, Pallas kernels, call(): pl.pallas_call(body, grid_spec=pltpu.PrefetchScalarGridSpec(num_scalar_pr...  272 us
    reduce_scatter x4, waiting for transfers between devices, reduce(): mine = lax.psum_scatter(grads, 'fsdp', scatter_dimension=0, tiled=True)[0]  201 us
    ppermute x8, waiting for transfers between devices, shift(): lax.ppermute(array, axis, [((i + by) % size, i) for i in range(size)])  78.9 us
    all_gather x3, waiting for transfers between devices, gather(): return lax.all_gather(packed, 'fsdp', axis=0, tiled=False)  60.8 us
  transfers between devices with their start and end apart: 15, of which 10 were waited for; matrix products, arithmetic and copies ran while one was open for 3% of the time, Pallas kernels for 9%

profile of v1, /device:TPU:0, one launch (start us, length us, event | category | flops | bytes accessed | tf_op | source)
XLA Modules:
  0.0 680.3 jit_solution(307520742972522792)
XLA Ops:
  7.2 5.4 concatenate.26
  16.5 1.5 pad_maximum_fusion.2
  22.8 3.0 collective-permute-start
  25.9 35.7 %all-gather.7.cloned.1.call-done = bf16[2304,512]{1,0:T(8,128)(2,1)} async-done(((bf16[144,512]{1,0:T(8,128)(2,1)}), bf16[2304,512]{1,0:T(8,128)(2,1)}) %all-gather.7.cloned.1.call-update) | async-done | bytes 2359312 | tf_op jit(solution)/shard_map/all_gather | solution.py:524
  62.8 1.4 copy.54.inner_bias
  64.9 7.7 %collective-permute-done = bf16[2,1024,512]{2,1,0:T(8,128)(2,1)} collective-permute-done((bf16[2,1024,512]{2,1,0:T(8,128)(2,1)}, bf16[2,1024,512]{2,1,0:T(8,128)(2,1)}, u32[]{:S(2)}, u32[]{:S(2)}) %collective-permute-start) | collective-permute-done | bytes 2097184 | tf_op jit(solution)/shard_map/ppermute | solution.py:515
  72.6 58.9 %shard_map.408 = (bf16[2,512,2048]{2,1,0:T(8,128)(2,1)}, bf16[2,512,2048]{2,1,0:T(8,128)(2,1)}, bf16[2,512,1024]{2,1,0:T(8,128)(2,1)}, bf16[2,512,1024]{2,1,0:T(...) custom-call(s32[2,8]{1,0:T(2,128)} %docs.3, ...), custom_call_target="tpu_custom_call" | custom-call | flops 6442450944 | bytes 33554432 | tf_op jit(solution)/shard_map/pallas_call | solution.py:499
  131.5 25.1 %all-gather.11.cloned.1.call-done = bf16[4096,512]{1,0:T(8,128)(2,1)} async-done(((bf16[256,512]{1,0:T(8,128)(2,1)}), bf16[4096,512]{1,0:T(8,128)(2,1)}) %all-gather.11.cloned.1.call-update) | async-done | bytes 4194320 | tf_op jit(solution)/shard_map/all_gather | solution.py:524
  156.6 109.5 %shard_map.409 = (bf16[2,512,1024]{2,1,0:T(8,128)(2,1)}, bf16[2,512,1024]{2,1,0:T(8,128)(2,1)}, bf16[2,512,1024]{2,1,0:T(8,128)(2,1)}, bf16[2,512,1024]{2,1,0:T(...) custom-call(f32[2,512,1024]{2,1,0:T(8,128)} %get-tuple-element.52.sc, ...), custom_call_target="tpu_custom_call" | custom-call | flops 32212254720 | bytes 33554432 | tf_op jit(solution)/shard_map/pallas_call | solution.py:499
  266.1 1.6 convert_reduce_fusion
  267.7 1.0 slice.136
  268.7 56.8 %shard_map.410 = (f32[2,512,1024]{2,1,0:T(8,128)}, bf16[2,512,1024]{2,1,0:T(8,128)(2,1)}, f32[2,512,512]{2,1,0:T(8,128)}, bf16[1,2,512,512]{3,2,1,0:T(8,128)(2,1...) custom-call(f32[2,512,1024]{2,1,0:T(8,128)} %get-tuple-element.54.second_grad, ...), custom_call_target="tpu_custom_call" | custom-call | flops 16106127360 | bytes 33554432 | tf_op jit(solution)/shard_map/pallas_call | solution.py:499
  325.6 1.0 slice.137
  327.0 46.8 %shard_map.411 = (f32[2,1024,512]{2,1,0:T(8,128)}, f32[2,1024,512]{2,1,0:T(8,128)}, bf16[1,2,1024,512]{3,2,1,0:T(8,128)(2,1)}, bf16[16,96,512]{2,1,0:T(8,128)(2,1)}) custom-call(s32[2,8]{1,0:T(2,128)} %docs.3, s32[1]{0:T(128)} %bitcast.place, bf16[2,1024,512]{2,1,0:T(8,128)(2,1)} %hidden.3, f32[2,512,1024]{2,1,0:T(8,128)} %get-tuple-element.63.first_grad, ...), custom_call_target="tpu_custom_call" | custom-call | flops 16106127360 | bytes 33554432 | tf_op jit(solution)/shard_map/pallas_call | solution.py:499
  373.8 2.8 pad_maximum_fusion
  377.9 1.8 collective-permute-start.2
  380.4 65.1 %collective-permute-done.3 = bf16[2,512,512]{2,1,0:T(8,128)(2,1)S(1)} collective-permute-done((bf16[2,512,512]{2,1,0:T(8,128)(2,1)S(1)}, bf16[2,512,512]{2,1,0:T(8,128)(2,1)S(1)}, u32[]{:S(2)}, u32[]{:S(2)}) %collective-permute-start.3) | collective-permute-done | bytes 1048608 | tf_op jit(solution)/shard_map/ppermute | solution.py:515
  445.5 3.3 convert_add_fusion.1
  448.8 21.8 %reduce-scatter.5.cloned.1.call-done = bf16[1,112,512]{2,1,0:T(8,128)(2,1)} async-done(((bf16[16,112,512]{2,1,0:T(8,128)(2,1)}), bf16[1,112,512]{2,1,0:T(8,128)(2,1)}) %reduce-scatter.5.cloned.1.call-update) | async-done | bytes 114704 | tf_op jit(solution)/shard_map/reduce_scatter | solution.py:691
  470.6 1.5 collective-permute-start.4
  472.1 5.0 convert_add_fusion
  478.3 56.5 %reduce-scatter.9.cloned.1.call-done = bf16[1,128,512]{2,1,0:T(8,128)(2,1)} async-done(((bf16[16,128,512]{2,1,0:T(8,128)(2,1)}), bf16[1,128,512]{2,1,0:T(8,128)(2,1)}) %reduce-scatter.9.cloned.1.call-update) | async-done | bytes 131088 | tf_op jit(solution)/shard_map/reduce_scatter | solution.py:691
  534.7 1.5 collective-permute-start.6
  536.8 62.6 %reduce-scatter.11.cloned.1.call-done = bf16[1,128,512]{2,1,0:T(8,128)(2,1)} async-done(((bf16[16,128,512]{2,1,0:T(8,128)(2,1)}), bf16[1,128,512]{2,1,0:T(8,128)(2,1)}) %reduce-scatter.11.cloned.1.call-update) | async-done | bytes 131088 | tf_op jit(solution)/shard_map/reduce_scatter | solution.py:691
  599.4 1.4 collective-permute-start.7
  600.9 0.9 convert_add_fusion.4
  601.8 2.8 collective-permute-done.7
  604.6 1.6 convert_add_fusion.3
  606.3 59.8 %reduce-scatter.7.cloned.1.call-done = bf16[1,160,512]{2,1,0:T(8,128)(2,1)} async-done(((bf16[16,160,512]{2,1,0:T(8,128)(2,1)}), bf16[1,160,512]{2,1,0:T(8,128)(2,1)}) %reduce-scatter.7.cloned.1.call-update) | async-done | bytes 163856 | tf_op jit(solution)/shard_map/reduce_scatter | solution.py:691
  666.1 1.5 collective-permute-start.5
  668.3 3.3 collective-permute-done.5
  671.6 1.0 convert_add_fusion.2
  (67 shorter events, 16.3 us)
Async XLA Ops:
  7.2 54.4 %all-gather.7.cloned.1.call-start = ((), (), s32[]{:S(2)}) async-start(), calls=%async_computation.8 | async-start | bytes 2506752 | tf_op jit(solution)/shard_map/all_gather | solution.py:524
  15.8 0.7 copy-start.1
  16.4 115.1 %all-gather.9.cloned.1.call-start = ((), (), s32[]{:S(2)}) async-start(), calls=%async_computation.9 | async-start | bytes 2228224 | tf_op jit(solution)/shard_map/all_gather | solution.py:524
  18.0 138.6 %all-gather.11.cloned.1.call-start = ((), (), s32[]{:S(2)}) async-start(), calls=%async_computation.10 | async-start | bytes 4456448 | tf_op jit(solution)/shard_map/all_gather | solution.py:524
  22.0 0.7 copy-start
  22.7 447.8 %reduce-scatter.5.cloned.1.call-start = ((), (), s32[]{:S(2)}) async-start(), calls=%async_computation.4 | async-start | bytes 1949696 | tf_op jit(solution)/shard_map/reduce_scatter | solution.py:691
  22.8 49.8 %collective-permute-start = (bf16[2,1024,512]{2,1,0:T(8,128)(2,1)}, bf16[2,1024,512]{2,1,0:T(8,128)(2,1)}, u32[]{:S(2)}, u32[]{:S(2)}) collective-permute-start(bf16[2,1024,512]{2,1,0:T(8,128)(2,1)} %own_tokens.3), channel_id=1, source_target_pairs={{1,0},{0,1},{3,2},{2,3},{5,4},{4,5},{7,6},{6,7},{9,8},{8,9},{11,10... | collective-permute-start | bytes 6291464 | tf_op jit(solution)/shard_map/ppermute | solution.py:515
  25.8 105.7 %collective-permute-start.1 = (bf16[2,512,512]{2,1,0:T(8,128)(2,1)}, bf16[2,512,512]{2,1,0:T(8,128)(2,1)S(1)}, u32[]{:S(2)}, u32[]{:S(2)}) collective-permute-start(bf16[2,512,512]{2,1,0:T(8,128)(2,1)} %own_enc.3), channel_id=1, source_target_pairs={{1,0},{0,1},{3,2},{2,3},{5,4},{4,5},{7,6},{6,7},{9,8},{8,9},{11,10... | collective-permute-start | bytes 3145736 | tf_op jit(solution)/shard_map/ppermute | solution.py:515
  131.5 25.1 %copy-start.4 = (bf16[2,512,512]{2,1,0:T(8,128)(2,1)}, bf16[2,512,512]{2,1,0:T(8,128)(2,1)S(1)}, u32[]{:S(2)}) copy-start(bf16[2,512,512]{2,1,0:T(8,128)(2,1)S(1)} %collective-permute-done.1) | copy-start | bytes 3145732
  376.7 158.1 %reduce-scatter.9.cloned.1.call-start = ((), (), s32[]{:S(2)}) async-start(), calls=%async_computation.6 | async-start | bytes 2228224 | tf_op jit(solution)/shard_map/reduce_scatter | solution.py:691
  377.2 222.2 %reduce-scatter.11.cloned.1.call-start = ((), (), s32[]{:S(2)}) async-start(), calls=%async_computation.7 | async-start | bytes 2228224 | tf_op jit(solution)/shard_map/reduce_scatter | solution.py:691
  377.3 2.4 copy-start.3
  377.8 288.3 %reduce-scatter.7.cloned.1.call-start = ((), (), s32[]{:S(2)}) async-start(), calls=%async_computation.5 | async-start | bytes 2785280 | tf_op jit(solution)/shard_map/reduce_scatter | solution.py:691
  377.9 94.2 %collective-permute-start.2 = (bf16[2,1024,512]{2,1,0:T(8,128)(2,1)}, bf16[2,1024,512]{2,1,0:T(8,128)(2,1)S(1)}, u32[]{:S(2)}, u32[]{:S(2)}) collective-permute-start(bf16[2,1024,512]{2,1,0:T(8,128)(2,1)} %bitcast.55), channel_id=1, source_target_pairs={{1,0},{0,1},{3,2},{2,3},{5,4},{4,5},{7,6},{6,7},{9,8},{8,9},{11,10... | collective-permute-start | bytes 6291464 | tf_op jit(solution)/shard_map/ppermute | solution.py:515
  379.7 65.8 %collective-permute-start.3 = (bf16[2,512,512]{2,1,0:T(8,128)(2,1)S(1)}, bf16[2,512,512]{2,1,0:T(8,128)(2,1)S(1)}, u32[]{:S(2)}, u32[]{:S(2)}) collective-permute-start(bf16[2,512,512]{2,1,0:T(8,128)(2,1)S(1)} %bitcast.56), channel_id=1, source_target_pairs={{1,0},{0,1},{3,2},{2,3},{5,4},{4,5},{7,6},{6,7},{9,8},{8,9},{11,10... | collective-permute-start | bytes 3145736 | tf_op jit(solution)/shard_map/ppermute | solution.py:515
  470.6 6.5 collective-permute-start.4
  472.1 5.0 copy-start.2
  534.7 66.1 %collective-permute-start.6 = (bf16[128,512]{1,0:T(8,128)(2,1)}, bf16[128,512]{1,0:T(8,128)(2,1)S(1)}, u32[]{:S(2)}, u32[]{:S(2)}) collective-permute-start(bf16[128,512]{1,0:T(8,128)(2,1)} %bitcast.44), channel_id=1, source_target_pairs={{1,0},{0,1},{3,2},{2,3},{5,4},{4,5},{7,6},{6,7},{9,8},{8,9},{11,10... | collective-permute-start | bytes 393224 | tf_op jit(solution)/shard_map/ppermute | solution.py:515
  599.4 5.2 collective-permute-start.7
  666.1 5.5 collective-permute-start.5
Sparse Core Ops, SparseCore 0:
  16.6 44.9 all-gather.6
  64.3 40.2 all-gather.8
  107.3 49.2 all-gather.10
  376.8 93.7 reduce-scatter.4
  474.2 60.5 reduce-scatter.8
  538.8 60.6 reduce-scatter.10
  603.2 62.8 reduce-scatter.6

commit v2 on v1

v2 whole, which is shorter than its diff:
```python
import functools
import math

import jax
import jax.numpy as jnp
from jax import lax
from jax.experimental import pallas as pl
from jax.experimental.pallas import tpu as pltpu
from jax.sharding import PartitionSpec as P

HD = 64
BLK = 256
WINDOW = 4
EPS = 1e-05
MASKED = -1e30
LOG2E = 1.4426950408889634
LN2 = 0.6931471805599453
SAFE = 60.0
F32 = jnp.float32
BF16 = jnp.bfloat16
NN = (((1,), (0,)), ((), ()))
NT = (((1,), (1,)), ((), ()))
TN = (((0,), (0,)), ((), ()))
VMEM_LIMIT = 62 * 2**20


def dot(left, right, form=NN):
    return lax.dot_general(left, right, form, preferred_element_type=F32)


def norm(rows):
    center = rows - jnp.mean(rows, axis=0, keepdims=True)
    inverse = lax.rsqrt(jnp.mean(center * center, axis=0, keepdims=True) + EPS)
    return center * inverse, inverse


def norm_back(scaled, inverse, gain, upstream):
    through = upstream * gain
    return inverse * (
        through
        - jnp.mean(through, axis=0, keepdims=True)
        - scaled * jnp.mean(through * scaled, axis=0, keepdims=True)
    )


def fold(values):
    total = values[:, :128]
    for start in range(128, values.shape[1], 128):
        total = total + values[:, start : start + 128]
    return total


def gelu_pair(x):
    size = jnp.abs(x)
    t = 1.0 / (1.0 + (0.3275911 / math.sqrt(2.0)) * size)
    bell = jnp.exp2((-0.5 * LOG2E) * (x * x))
    series = t * (
        0.127414796 + t * (-0.142248368 + t * (0.7107068705 + t * (-0.7265760135 + t * 0.5307027145)))
    )
    tail = series * bell
    phi = jnp.where(x >= 0.0, 1.0 - tail, tail)
    return x * phi, phi + x * bell * (1.0 / math.sqrt(2.0 * math.pi))


def owner_of(spot, m, d, depth):
    z = lax.rem(spot[1] + d, depth)
    return (z * 2 + jnp.bitwise_xor(spot[2], m // 2)) * 2 + jnp.bitwise_xor(spot[3], m % 2)


def unpack(packs, spot, first, rows, plain):
    for m, pack in enumerate(packs):
        depth = pack.shape[0]
        for d in range(depth):
            at = pl.ds(pl.multiple_of(owner_of(spot, m, d, depth) * rows, rows), rows)
            plain[at, :] = pack[d, first : first + rows, :]


def send_grad(outs, spot, first, rows, acc, masks=(0, 1, 2, 3)):
    depth = outs[0].shape[0]
    for out, m in zip(outs, masks):
        for d in range(depth):
            at = pl.ds(pl.multiple_of(owner_of(spot, m, d, depth) * rows, rows), rows)
            out[d, first : first + rows, :] = acc[at, :].astype(BF16)


def attend(count, exact, keys, values, off, query, probs, mixed, inverse, bias):
    head_count = query.shape[0] // HD

    def scores(hs, j):
        part = dot(keys[hs, pl.ds(off + j * BLK, BLK)], query[hs, :], TN)
        if bias is not None:
            part = part + bias[j * BLK : (j + 1) * BLK, :]
        return part

    def first(h, hs):
        total = None
        if exact:
            parts = [scores(hs, j) for j in range(count)]
            top = jnp.max(parts[0], axis=0, keepdims=True)
            for part in parts[1:]:
                top = jnp.maximum(top, jnp.max(part, axis=0, keepdims=True))
        for j in range(count):
            terms = jnp.exp2(parts[j] - top if exact else scores(hs, j))
            partial = jnp.sum(terms.reshape(BLK // 8, 8, BLK), axis=0)
            total = partial if total is None else total + partial
            probs[h, j * BLK : (j + 1) * BLK, :] = terms.astype(BF16)
        return total

    def second(h, hs, total):
        sums = dot(values[hs, pl.ds(off, count * BLK)], probs[h, : count * BLK, :])
        scale = 1.0 / jnp.sum(total, axis=0, keepdims=True)
        mixed[hs, :] = (sums * scale).astype(BF16)
        inverse[pl.ds(h, 1), :] = scale

    if exact:

        def one(h, carry):
            hs = pl.ds(pl.multiple_of(h * HD, HD), HD)
            second(h, hs, first(h, hs))
            return carry

        lax.fori_loop(0, head_count, one, 0)
        return
    waiting = None
    for h in range(head_count):
        total = first(h, slice(h * HD, (h + 1) * HD))
        if h > 0:
            second(h - 1, slice((h - 1) * HD, h * HD), waiting)
        waiting = total
    second(head_count - 1, slice((head_count - 1) * HD, head_count * HD), waiting)


def attend_back(
    count, keys, values, off, query, grad, inner, probs, kept, query_grad, key_grad, value_grad
):
    head_count = query.shape[0] // HD

    def first(h):
        hs = slice(h * HD, (h + 1) * HD)
        for j in range(count):
            us = slice(j * BLK, (j + 1) * BLK)
            prob_grad = dot(values[hs, pl.ds(off + j * BLK, BLK)], grad[hs, :], TN)
            kept[h, us, :] = (probs[h, us, :].astype(F32) * (prob_grad - inner[h : h + 1, :])).astype(BF16)

    def second(h):
        hs = slice(h * HD, (h + 1) * HD)
        us = slice(0, count * BLK)
        window = pl.ds(off, count * BLK)
        query_grad[hs, :] = (dot(keys[hs, window], kept[h, us, :]) * (1.0 / math.sqrt(HD))).astype(BF16)
        key_grad[hs, window] += dot(query[hs, :], kept[h, us, :], NT)
        value_grad[hs, window] += dot(grad[hs, :], probs[h, us, :], NT)

    first(0)
    for h in range(1, head_count):
        first(h)
        second(h - 1)
    second(head_count - 1)


def scale_grad(mixed_grad, mixed, inverse, grad, inner):
    for h in range(mixed.shape[0] // HD):
        hs = slice(h * HD, (h + 1) * HD)
        scaled = mixed_grad[hs, :] * inverse[h : h + 1, :]
        grad[hs, :] = scaled.astype(BF16)
        inner[h : h + 1, :] = jnp.sum(scaled * mixed[hs, :].astype(F32), axis=0, keepdims=True)


def head_norms(rows, head_count):
    found = []
    for h in range(head_count):
        part = rows[h * HD : (h + 1) * HD, :].astype(F32)
        found.append(jnp.max(jnp.sum(part * part, axis=0, keepdims=True), axis=1, keepdims=True))
    return found


def safe_scores(query, key_norms):
    head_count = query.shape[0] // HD
    worst = None
    for h, found in enumerate(head_norms(query[...], head_count)):
        product = found * key_norms[h : h + 1, 0:1]
        worst = product if worst is None else jnp.maximum(worst, product)
    return jnp.max(worst) < SAFE * SAFE


def store_key_norms(key_norms, keys):
    head_count = keys.shape[0] // HD
    for h, found in enumerate(head_norms(keys[...], head_count)):
        key_norms[h : h + 1, :] = jnp.broadcast_to(found, (1, key_norms.shape[1]))


def doc_span(docs, seq, block, block_count):
    mine = docs[seq, block]
    low = jnp.int32(0)
    count = jnp.int32(0)
    for b in range(block_count):
        low = low + jnp.where(docs[seq, b] < mine, 1, 0).astype(jnp.int32)
        count = count + jnp.where(docs[seq, b] == mine, 1, 0).astype(jnp.int32)
    return low, count


def self_forward_kernel(
    shard, docs, spot, hidden, own_tokens, far_tokens, order, reach, pack0, pack1, pack2, pack3,
    keys, values, query, mixed, probs, inverse,
    plain, q_turned, k_turned, v_turned, bias, key_norms,
):
    seq, step = pl.program_id(0), pl.program_id(1)
    steps = pl.num_programs(1)
    rows = shard
    local = own_tokens.shape[1]
    far = far_tokens.shape[2]
    parts = far_tokens.shape[0] + 1
    block_count = order.shape[1]
    me = spot[0]

    @pl.when((seq == 0) & (step == 0))
    def _():
        for which, turned in enumerate((q_turned, k_turned, v_turned)):
            unpack((pack0, pack1, pack2, pack3), spot, which * rows, rows, plain.at[which])
            turned[...] = plain[which].T

    @pl.when(step == 0)
    def _():
        if far != local:
            keys[...] = jnp.zeros_like(keys)
        for part in range(parts):
            tokens = own_tokens[0] if part == 0 else far_tokens[part - 1, 0]
            at = token_window(me, part, parts, local, far)
            turned = tokens.T
            keys[0, :, at] = dot(k_turned[...], turned).astype(BF16)
            values[0, :, at] = dot(v_turned[...], turned).astype(BF16)
        store_key_norms(key_norms, keys.at[0])

    block = me * steps + step
    low, count = doc_span(docs, seq, block, block_count)
    query[0] = (dot(q_turned[...], hidden[0].T) * (LOG2E / math.sqrt(HD))).astype(BF16)

    order_turned = order[0].astype(F32).T
    lanes = lax.broadcasted_iota(jnp.int32, order_turned.shape, 1)
    reach_row = reach[0, pl.ds(block, 1), :].astype(F32)
    differ = lax.broadcasted_iota(jnp.int32, (BLK, BLK), 0) != lax.broadcasted_iota(
        jnp.int32, (BLK, BLK), 1
    )
    for j in range(WINDOW):
        at = low + j
        column = jnp.sum(jnp.where(lanes == at, order_turned, 0.0), axis=1, keepdims=True)
        seen = (column < reach_row) & (differ | (at != block))
        bias[j * BLK : (j + 1) * BLK, :] = jnp.where(seen, 0.0, MASKED)

    safe = safe_scores(query.at[0], key_norms)
    off = pl.multiple_of(low * BLK, BLK)
    for size in range(1, WINDOW + 1):
        for exact in (False, True):

            @pl.when((count == size) & (safe != exact))
            def _(size=size, exact=exact):
                attend(
                    size, exact, keys.at[0], values.at[0], off, query.at[0], probs.at[0, 0],
                    mixed.at[0], inverse.at[0, 0], bias,
                )


def token_window(me, part, parts, local, far):
    owner = lax.rem(me + part, parts)
    if part == 0 or far == local:
        return pl.ds(pl.multiple_of(owner * local, BLK), local)
    return pl.ds(pl.multiple_of(owner * local + jnp.where(owner == 0, local - far, 0), BLK), far)


def cross_forward_kernel(
    shard, bias_rows, spot, hidden, self_mixed, own_enc, far_enc, pack0, pack1, pack2, pack3,
    keys, values, query, mixed, probs, inverse, scaled1, scaled2, inverses, cols, bias_col,
    plain, spread_rows, so_turned, q_turned, k_turned, v_turned, o_turned, key_norms,
):
    seq, step = pl.program_id(0), pl.program_id(1)
    rows = shard
    local = own_enc.shape[1]
    parts = far_enc.shape[0] + 1
    packs = (pack0, pack1, pack2, pack3)

    @pl.when((seq == 0) & (step == 0))
    def _():
        for which, turned in enumerate((so_turned, q_turned, k_turned, v_turned, o_turned)):
            unpack(packs, spot, which * rows, rows, plain.at[which])
            turned[...] = plain[which].T
        depth = pack0.shape[0]
        for m, pack in enumerate(packs):
            for d in range(depth):
                row = pack[d, 5 * rows : 5 * rows + 16, :].astype(F32)[0:1, :]
                spread_rows[pl.ds(owner_of(spot, m, d, depth), 1), :] = row
        spread = spread_rows[...].T
        count = 4 * depth
        bias_col[...] = jnp.concatenate([spread[:bias_rows, f : f + 1] for f in range(count)], axis=0)
        for v in range(7):
            at = slice(bias_rows + v * rows, bias_rows + (v + 1) * rows)
            cols[:, v : v + 1] = jnp.concatenate([spread[at, f : f + 1] for f in range(count)], axis=0)

    @pl.when(step == 0)
    def _():
        for part in range(parts):
            turned = (own_enc[0] if part == 0 else far_enc[part - 1, 0]).T
            at = slice(part * local, (part + 1) * local)
            keys[0, :, at] = dot(k_turned[...], turned).astype(BF16)
            values[0, :, at] = dot(v_turned[...], turned).astype(BF16)
        store_key_norms(key_norms, keys.at[0])

    center, inverse1 = norm(hidden[0].T.astype(F32) + dot(so_turned[...], self_mixed[0]))
    scaled1[0] = center
    normed = center * cols[:, 0:1] + cols[:, 1:2]
    query[0] = (dot(q_turned[...], normed.astype(BF16)) * (LOG2E / math.sqrt(HD))).astype(BF16)
    safe = safe_scores(query.at[0], key_norms)
    for exact in (False, True):

        @pl.when(safe != exact)
        def _(exact=exact):
            attend(
                parts * local // BLK, exact, keys.at[0], values.at[0], 0, query.at[0], probs.at[0, 0],
                mixed.at[0], inverse.at[0, 0], None,
            )

    normed = scaled1[0] * cols[:, 0:1] + cols[:, 1:2]
    center, inverse2 = norm(normed + dot(o_turned[...], mixed[0]))
    scaled2[0] = center
    inverses[0, 0, 0:1, :] = inverse1
    inverses[0, 0, 1:2, :] = inverse2


def feed_forward_kernel(
    shard, outer_rows, spot, scaled2_in, inverses, out_grad, pack0, pack1, pack2, pack3, cols, inner_bias,
    second_grad, layer_out, out0, out1, out2, out3, late,
    inner, inner_turned, outer, outer_turned, inner_acc, outer_acc, sums, bias_sum, slope, sheet,
):
    seq, step = pl.program_id(0), pl.program_id(1)
    rows = shard
    first_step = (seq == 0) & (step == 0)
    last_step = (seq == pl.num_programs(0) - 1) & (step == pl.num_programs(1) - 1)
    width = inner.shape[0]
    chunks = inner.shape[1] // width
    packs = (pack0, pack1, pack2, pack3)

    @pl.when(first_step)
    def _():
        for c in range(chunks):
            cs = slice(c * width, (c + 1) * width)
            unpack(packs, spot, c * rows, rows, inner.at[:, cs])
            inner_turned[cs, :] = inner[:, cs].T
        unpack(packs, spot, chunks * rows, outer_rows, outer)
        for c in range(chunks):
            cs = slice(c * width, (c + 1) * width)
            outer_turned[:, cs] = outer[cs, :].T
        inner_acc[...] = jnp.zeros_like(inner_acc)
        outer_acc[...] = jnp.zeros_like(outer_acc)
        sums[...] = jnp.zeros_like(sums)
        bias_sum[...] = jnp.zeros_like(bias_sum)

    scaled2 = scaled2_in[0]
    gain2 = cols[:, 2:3]
    middle = scaled2 * gain2 + cols[:, 3:4]
    middle_low = middle.astype(BF16)
    pre = dot(inner_turned[...], middle_low) + inner_bias[...]
    active, pull = gelu_pair(pre)
    active = active.astype(BF16)
    slope[...] = pull.astype(BF16)
    third_sum = middle + dot(outer_turned[...], active) + cols[:, 6:7]
    scaled3, inverse3 = norm(third_sum)
    gain3 = cols[:, 4:5]
    layer_out[0] = (scaled3 * gain3 + cols[:, 5:6]).T
    upstream = out_grad[0].T.astype(F32)
    third_grad = norm_back(scaled3, inverse3, gain3, upstream)
    sums[2] += fold(upstream * scaled3)
    sums[3] += fold(upstream)
    outer_low = third_grad.astype(BF16)
    sums[4] += fold(outer_low.astype(F32))
    outer_acc[...] += dot(active, outer_low, NT)
    inner_low = (dot(outer[...], outer_low) * slope[...].astype(F32)).astype(BF16)
    bias_sum[...] += fold(inner_low.astype(F32))
    inner_acc[...] += dot(middle_low, inner_low, NT)
    middle_grad = third_grad + dot(inner[...], inner_low)
    sums[0] += fold(middle_grad * scaled2)
    sums[1] += fold(middle_grad)
    second_grad[0] = norm_back(scaled2, inverses[0, 0, 1:2, :], gain2, middle_grad)

    @pl.when(last_step)
    def _():
        outs = (out0, out1, out2, out3)
        for c in range(chunks):
            send_grad(outs, spot, c * rows, rows, inner_acc.at[:, c * width : (c + 1) * width])
        send_grad(outs, spot, chunks * rows, outer_rows, outer_acc)
        sheet[...] = jnp.zeros_like(sheet)
        for which in range(5):
            sheet[:, which : which + 1] = jnp.sum(sums[which], axis=1, keepdims=True)
        for c in range(chunks):
            part = bias_sum[c * width : (c + 1) * width, :]
            sheet[:, 8 + c : 9 + c] = jnp.sum(part, axis=1, keepdims=True)
        late[...] = sheet[...].T[0:16, :]


def cross_back_kernel(
    shard, spot, second_grad, scaled1, inverses, own_enc, far_enc, keys, values, query, mixed, probs, inverse,
    self_mixed, pack0, pack1, pack2, pack3, cols, late,
    first_grad, self_mixed_grad, own_part, far_part, out0, out1,
    so_plain, q_plain, k_plain, v_plain, o_plain, accs, sums, sheet,
    key_acc, value_acc, kept, grad, inner, query_grad,
):
    seq, step = pl.program_id(0), pl.program_id(1)
    rows = shard
    first_step = (seq == 0) & (step == 0)
    last_step = (seq == pl.num_programs(0) - 1) & (step == pl.num_programs(1) - 1)
    local = own_enc.shape[1]
    parts = far_enc.shape[0] + 1

    @pl.when(first_step)
    def _():
        for which, plain in enumerate((so_plain, q_plain, k_plain, v_plain, o_plain)):
            unpack((pack0, pack1, pack2, pack3), spot, which * rows, rows, plain)
        accs[...] = jnp.zeros_like(accs)
        sums[...] = jnp.zeros_like(sums)

    @pl.when(step == 0)
    def _():
        key_acc[...] = jnp.zeros_like(key_acc)
        value_acc[...] = jnp.zeros_like(value_acc)

    cross_low = second_grad[0].astype(BF16)
    scale_grad(dot(o_plain[...], cross_low), mixed.at[0], inverse.at[0, 0], grad, inner)
    accs[4] += dot(mixed[0], cross_low, NT)
    attend_back(
        parts * local // BLK, keys.at[0], values.at[0], 0, query.at[0], grad, inner, probs.at[0, 0],
        kept, query_grad, key_acc, value_acc,
    )
    scaled = scaled1[0]
    gain = cols[:, 0:1]
    normed_low = (scaled * gain + cols[:, 1:2]).astype(BF16)
    accs[1] += dot(normed_low, query_grad[...], NT)
    normed_grad = second_grad[0] + dot(q_plain[...], query_grad[...])
    sums[0] += fold(normed_grad * scaled)
    sums[1] += fold(normed_grad)
    through = norm_back(scaled, inverses[0, 0, 0:1, :], gain, normed_grad)
    first_grad[0] = through
    self_low = through.astype(BF16)
    accs[0] += dot(self_mixed[0], self_low, NT)
    self_mixed_grad[0] = dot(so_plain[...], self_low).astype(BF16)

    @pl.when(step == pl.num_programs(1) - 1)
    def _():
        for part in range(parts):
            at = slice(part * local, (part + 1) * local)
            key_low = (key_acc[:, at] * LN2).astype(BF16)
            value_low = value_acc[:, at].astype(BF16)
            turned = (own_enc[0] if part == 0 else far_enc[part - 1, 0]).T
            accs[2] += dot(turned, key_low, NT)
            accs[3] += dot(turned, value_low, NT)
            whole = (dot(k_plain[...], key_low) + dot(v_plain[...], value_low)).T
            if part == 0:
                own_part[0] = whole
            else:
                far_part[part - 1, 0] = whole.astype(BF16)

    @pl.when(last_step)
    def _():
        for y in range(2):
            outs = (out0.at[y], out1.at[y])
            for which in range(5):
                send_grad(outs, spot, which * rows, rows, accs.at[which], (2 * y, 2 * y + 1))
        sheet[...] = jnp.zeros_like(sheet)
        for which in range(2):
            sheet[:, 5 + which : 6 + which] = jnp.sum(sums[which], axis=1, keepdims=True)
        tray = (sheet[...].T[0:16, :] + late[...]).astype(BF16)
        for out in (out0, out1):
            for y in range(2):
                for d in range(out.shape[1]):
                    out[y, d, 5 * rows : 5 * rows + 16, :] = tray


def self_back_kernel(
    shard, docs, spot, hidden, first_grad, own_tokens, far_tokens, keys, values, query, mixed, probs, inverse,
    mixed_grad, pack0, pack1, pack2, pack3,
    hidden_grad, own_part, far_part, out0, out1,
    accs, q_plain, k_plain, v_plain, key_acc, value_acc, kept, grad, inner, query_grad,
):
    seq, step = pl.program_id(0), pl.program_id(1)
    steps = pl.num_programs(1)
    rows = shard
    local = own_tokens.shape[1]
    far = far_tokens.shape[2]
    parts = far_tokens.shape[0] + 1
    me = spot[0]
    block_count = parts * steps

    @pl.when((seq == 0) & (step == 0))
    def _():
        for which, plain in enumerate((q_plain, k_plain, v_plain)):
            unpack((pack0, pack1, pack2, pack3), spot, which * rows, rows, plain)
        accs[...] = jnp.zeros_like(accs)

    @pl.when(step == 0)
    def _():
        key_acc[...] = jnp.zeros_like(key_acc)
        value_acc[...] = jnp.zeros_like(value_acc)

    low, count = doc_span(docs, seq, me * steps + step, block_count)
    off = pl.multiple_of(low * BLK, BLK)
    scale_grad(mixed_grad[0].astype(F32), mixed.at[0], inverse.at[0, 0], grad, inner)
    for size in range(1, WINDOW + 1):

        @pl.when(count == size)
        def _(size=size):
            attend_back(
                size, keys.at[0], values.at[0], off, query.at[0], grad, inner, probs.at[0, 0],
                kept, query_grad, key_acc, value_acc,
            )

    accs[0] += dot(hidden[0].T, query_grad[...], NT)
    hidden_grad[0] = (first_grad[0] + dot(q_plain[...], query_grad[...])).T

    @pl.when(step == steps - 1)
    def _():
        for part in range(parts):
            at = token_window(me, part, parts, local, far)
            key_low = (key_acc[:, at] * LN2).astype(BF16)
            value_low = value_acc[:, at].astype(BF16)
            turned = (own_tokens[0] if part == 0 else far_tokens[part - 1, 0]).T
            accs[1] += dot(turned, key_low, NT)
            accs[2] += dot(turned, value_low, NT)
            whole = (dot(k_plain[...], key_low) + dot(v_plain[...], value_low)).T
            if part == 0:
                own_part[0] = whole
            else:
                far_part[part - 1, 0] = whole.astype(BF16)

    @pl.when((seq == pl.num_programs(0) - 1) & (step == steps - 1))
    def _():
        for y in range(2):
            outs = (out0.at[y], out1.at[y])
            for which in range(3):
                send_grad(outs, spot, which * rows, rows, accs.at[which], (2 * y, 2 * y + 1))


def settle_kernel(spot, own, far, out):
    out[...] = own[...] + far[...].astype(F32)


def whole_spec():
    return pl.BlockSpec(memory_space=pltpu.VMEM)


def call(body, grid, scalars, in_specs, out_specs, out_shape, scratch, micros, args, aliases={}):
    return pl.pallas_call(
        body,
        grid_spec=pltpu.PrefetchScalarGridSpec(
            num_scalar_prefetch=scalars,
            grid=grid,
            in_specs=in_specs,
            out_specs=out_specs,
            scratch_shapes=scratch,
        ),
        out_shape=[jax.ShapeDtypeStruct(shape, kind) for shape, kind in out_shape],
        input_output_aliases=aliases,
        compiler_params=pltpu.CompilerParams(vmem_limit_bytes=VMEM_LIMIT),
        cost_estimate=pl.CostEstimate(flops=int(micros * 1e9), bytes_accessed=2**24, transcendentals=0),
    )(*args)


def shift(array, axis, by, size):
    return lax.ppermute(array, axis, [((i + by) % size, i) for i in range(size)])


def z_shift(array, by, depth):
    pairs = [(((z + by) % depth) * 4 + w, z * 4 + w) for z in range(depth) for w in range(4)]
    return lax.ppermute(array, "fsdp", pairs)


def w_flip(array, mask, depth):
    return lax.ppermute(array, "fsdp", [(z * 4 + (w ^ mask), z * 4 + w) for z in range(depth) for w in range(4)])


def together(*arrays):
    return lax.optimization_barrier(arrays)


def after(array, *earlier):
    return lax.optimization_barrier((array,) + earlier)[0]


def gather_stack(packed, got):
    return jnp.stack([packed] + got)


def gather_z(packed, depth):
    return gather_stack(packed, [z_shift(packed, d, depth) for d in range(1, depth)])


def gather_w(pieces, depth):
    across = w_flip(pieces, 2, depth)
    return [pieces, w_flip(pieces, 1, depth), across, w_flip(across, 1, depth)]


def swap_w(outs, depth):
    return [w_flip(outs[m], m, depth) for m in (1, 2, 3)]


def swap_z(pieces, depth):
    return [z_shift(pieces[d].astype(BF16), -d, depth) for d in range(1, depth)]


def add_w(own, got, depth):
    return [sum(piece[d].astype(F32) for piece in [own] + got) for d in range(depth)]


def swap_sp(total, sp):
    mine = total.astype(BF16)
    return [shift(mine, "sp", r, sp) for r in range(1, sp)]


def add_all(total, got):
    return sum((piece.astype(F32) for piece in got), total)


def on_device(sp, fsdp, *arrays):
    (
        hidden_in, token_stream, encoder_out, out_grad, doc_ids, key_order, context_size,
        self_query, self_key, self_value, self_output, cross_query, cross_key, cross_value, cross_output,
        inner_weight, inner_bias, outer_weight, outer_bias, first_gain, first_shift, second_gain,
        second_shift, third_gain, third_shift,
    ) = arrays
    seqs, local, width = hidden_in.shape
    enc_local = encoder_out.shape[1]
    shard, hidden_width = inner_weight.shape
    outer_rows = outer_weight.shape[0]
    bias_rows = inner_bias.shape[0]
    chunks = hidden_width // width
    steps = local // BLK
    heads = width // HD
    length = local * sp
    enc_len = enc_local * sp
    block_count = key_order.shape[1]
    depth = fsdp // 4
    tray = 16
    far = min(local, (WINDOW - 1) * BLK) if sp == 2 else local

    me, mine = lax.axis_index("sp"), lax.axis_index("fsdp")
    spot = jnp.stack([me, mine // 4, mine // 2 % 2, mine % 2]).astype(jnp.int32)

    pack_a = jnp.concatenate([self_query, self_key, self_value], axis=0)
    sent = token_stream
    if far != local:
        start = jnp.where(me == 0, local - far, 0)
        sent = lax.dynamic_slice(token_stream, (0, start, 0), (seqs, far, width))
    far_tokens = jnp.stack([shift(sent, "sp", r, sp) for r in range(1, sp)])
    vectors = (inner_bias, first_gain, first_shift, second_gain, second_shift, third_gain, third_shift, outer_bias)
    flat = jnp.concatenate(vectors)
    flat = jnp.pad(flat, (0, tray * width - flat.shape[0])).reshape(tray, width)
    pack_b = jnp.concatenate([self_output, cross_query, cross_key, cross_value, cross_output, flat], axis=0)
    pack_c = jnp.concatenate(jnp.split(inner_weight, chunks, axis=1) + [outer_weight], axis=0)

    pieces_a = gather_z(pack_a, depth)
    pieces_b = gather_z(after(pack_b, pieces_a), depth)
    packs_a = gather_w(pieces_a, depth)
    hidden_early, pieces_b = together(hidden_in, pieces_b)
    core_b = w_flip(pieces_b, 1, depth)
    hidden_early, core_b = together(hidden_early, core_b)
    swap_b = w_flip(pieces_b, 2, depth)
    swap_c = [z_shift(after(pack_c, pieces_b), d, depth) for d in range(1, depth)]
    sent = after(encoder_out, far_tokens)
    far_enc = jnp.stack([shift(sent, "sp", r, sp) for r in range(1, sp)])

    whole = whole_spec()
    anywhere = pl.BlockSpec(memory_space=pl.ANY)
    turned_spec = lambda b=0: pl.BlockSpec((1, width, BLK), lambda s, i, *_: (s + b, 0, i))
    plain_spec = lambda b=0: pl.BlockSpec((1, BLK, width), lambda s, i, *_: (s + b, i, 0))
    per_seq = lambda shape, b=0: pl.BlockSpec((1,) + shape, lambda s, i, *_: (s + b, 0, 0))
    far_seq = lambda rows: pl.BlockSpec((sp - 1, 1, rows, width), lambda s, i, *_: (0, s, 0, 0))
    rows_spec = lambda b=0: pl.BlockSpec((1, 1, 8, BLK), lambda s, i, *_: (s + b, i, 0, 0))
    probs_spec = lambda keys, b=0: pl.BlockSpec(
        (1, 1, heads, keys, BLK), lambda s, i, *_: (s + b, i, 0, 0, 0)
    )
    turned_shape = (seqs, width, local)
    rows_shape = (seqs, steps, 8, BLK)
    big = lambda a, b, kind: pltpu.VMEM((a, b), kind)
    square = big(width, width, BF16)
    window = WINDOW * BLK

    keys, values, query, mixed, probs, inverse = call(
        functools.partial(self_forward_kernel, shard),
        (seqs, steps), 2,
        [
            plain_spec(), per_seq((local, width)), far_seq(far), per_seq((block_count, BLK)),
            per_seq((block_count, BLK)),
        ] + [whole] * 4,
        [
            per_seq((width, length)), per_seq((width, length)), turned_spec(), turned_spec(),
            probs_spec(window), rows_spec(),
        ],
        [
            ((seqs, width, length), BF16), ((seqs, width, length), BF16), (turned_shape, BF16),
            (turned_shape, BF16), ((seqs, steps, heads, window, BLK), BF16), (rows_shape, F32),
        ],
        [pltpu.VMEM((3, width, width), BF16)] + [square] * 3 + [big(window, BLK, F32), big(heads, 128, F32)],
        32000.0,
        (doc_ids, spot, hidden_early, token_stream, far_tokens, key_order, context_size, *packs_a),
    )
    keys, values, query, mixed, probs, inverse, pieces_b, far_enc, swap_b, *swap_c = together(
        keys, values, query, mixed, probs, inverse, pieces_b, far_enc, swap_b, *swap_c
    )
    packs_b = [pieces_b, core_b, swap_b, w_flip(swap_b, 1, depth)]
    pieces_c = jnp.stack([pack_c] + swap_c)
    mixed, pieces_c = together(mixed, pieces_c)
    swap_c = w_flip(pieces_c, 2, depth)

    (
        cross_keys, cross_values, cross_q, cross_mixed, cross_probs, cross_inverse, scaled1, scaled2, inverses,
        cols, inner_bias_col,
    ) = call(
        functools.partial(cross_forward_kernel, shard, bias_rows),
        (seqs, steps), 1,
        [plain_spec(), turned_spec(), per_seq((enc_local, width)), far_seq(enc_local)] + [whole] * 4,
        [
            per_seq((width, enc_len)), per_seq((width, enc_len)), turned_spec(), turned_spec(), probs_spec(enc_len),
            rows_spec(), turned_spec(), turned_spec(), rows_spec(), whole, whole,
        ],
        [
            ((seqs, width, enc_len), BF16), ((seqs, width, enc_len), BF16), (turned_shape, BF16),
            (turned_shape, BF16), ((seqs, steps, heads, enc_len, BLK), BF16), (rows_shape, F32),
            (turned_shape, F32), (turned_shape, F32), (rows_shape, F32), ((width, 8), F32),
            ((hidden_width, 1), F32),
        ],
        [pltpu.VMEM((5, width, width), BF16), big(fsdp, width, F32)] + [square] * 5 + [big(heads, 128, F32)],
        32000.0,
        (spot, hidden_in, mixed, encoder_out, far_enc, *packs_b),
    )

    (
        cross_keys, cross_values, cross_q, cross_mixed, cross_probs, cross_inverse, scaled1, scaled2, inverses,
        cols, inner_bias_col, pieces_c, swap_c,
    ) = together(
        cross_keys, cross_values, cross_q, cross_mixed, cross_probs, cross_inverse, scaled1, scaled2, inverses,
        cols, inner_bias_col, pieces_c, swap_c,
    )
    packs_c = [pieces_c, w_flip(pieces_c, 1, depth), swap_c, w_flip(swap_c, 1, depth)]

    grads_shape = lambda rows: [((depth, rows, width), BF16)] * 4
    ff_rows = chunks * shard + outer_rows
    second_grad, layer_out, *ff_outs, late = call(
        functools.partial(feed_forward_kernel, shard, outer_rows),
        (seqs, steps), 1,
        [turned_spec(), rows_spec(), plain_spec()] + [whole] * 6,
        [turned_spec(), plain_spec()] + [whole] * 5,
        [(turned_shape, F32), ((seqs, local, width), F32)] + grads_shape(ff_rows) + [((16, width), F32)],
        [
            big(width, hidden_width, BF16), big(hidden_width, width, BF16), big(hidden_width, width, BF16),
            big(width, hidden_width, BF16), big(width, hidden_width, F32), big(hidden_width, width, F32),
            pltpu.VMEM((5, width, 128), F32), big(hidden_width, 128, F32), big(hidden_width, BLK, BF16),
            big(width, 128, F32),
        ],
        70000.0,
        (spot, scaled2, inverses, out_grad, *packs_c, cols, inner_bias_col),
    )

    ff_swap = swap_w(ff_outs, depth)
    attention_scratch = lambda keys_len, kept_len: [
        big(width, keys_len, F32), big(width, keys_len, F32), pltpu.VMEM((heads, kept_len, BLK), BF16),
        big(width, BLK, BF16), big(heads, BLK, F32), big(width, BLK, BF16),
    ]
    first_grad, mixed_grad, own_enc_part, far_enc_part, *cross_outs = call(
        functools.partial(cross_back_kernel, shard),
        (seqs, steps), 1,
        [
            turned_spec(), turned_spec(), rows_spec(), per_seq((enc_local, width)), far_seq(enc_local),
            per_seq((width, enc_len)), per_seq((width, enc_len)), turned_spec(), turned_spec(),
            probs_spec(enc_len), rows_spec(), turned_spec(),
        ] + [whole] * 6,
        [
            turned_spec(), turned_spec(), per_seq((enc_local, width)), far_seq(enc_local),
        ] + [whole] * 2,
        [
            (turned_shape, F32), (turned_shape, BF16), ((seqs, enc_local, width), F32),
            ((sp - 1, seqs, enc_local, width), BF16),
        ] + [((2, depth, 5 * shard + tray, width), BF16)] * 2,
        [square] * 5
        + [pltpu.VMEM((5, width, width), F32), pltpu.VMEM((2, width, 128), F32), big(width, 128, F32)]
        + attention_scratch(enc_len, enc_len),
        56000.0,
        (
            spot, second_grad, scaled1, inverses, encoder_out, far_enc, cross_keys, cross_values, cross_q,
            cross_mixed, cross_probs, cross_inverse, mixed, *packs_b, cols, late,
        ),
    )

    first_grad, mixed_grad, own_enc_part, far_enc_part, *got = together(
        first_grad, mixed_grad, own_enc_part, far_enc_part, *cross_outs, *ff_swap
    )
    cross_outs, ff_swap = got[:2], got[2:]
    cross_core = w_flip(cross_outs[1], 1, depth)
    ff_pieces = add_w(ff_outs[0], ff_swap, depth)
    cross_half = [cross_outs[0][y].astype(F32) + cross_core[y].astype(F32) for y in range(2)]
    mixed_grad, *got = together(mixed_grad, *cross_half, *ff_pieces)
    cross_half, ff_pieces = got[:2], got[2:]
    ff_swap = swap_z(ff_pieces, depth)
    enc_swap = [shift(far_enc_part[r - 1], "sp", -r, sp) for r in range(1, sp)]
    cross_swap = w_flip(cross_half[1].astype(BF16), 2, depth)
    hidden_grad, token_grad, far_part, *self_outs = call(
        functools.partial(self_back_kernel, shard),
        (seqs, steps), 2,
        [
            plain_spec(), turned_spec(), per_seq((local, width)), far_seq(far),
            per_seq((width, length)), per_seq((width, length)), turned_spec(), turned_spec(),
            probs_spec(window), rows_spec(), turned_spec(),
        ] + [whole] * 4,
        [plain_spec(), per_seq((local, width)), far_seq(far)] + [whole] * 2,
        [((seqs, local, width), F32), ((seqs, local, width), F32), ((sp - 1, seqs, far, width), BF16)]
        + [((2, depth, 3 * shard, width), BF16)] * 2,
        [pltpu.VMEM((3, width, width), F32)] + [square] * 3 + attention_scratch(length, window),
        50000.0,
        (
            doc_ids, spot, hidden_in, first_grad, token_stream, far_tokens, keys, values, query, mixed,
            probs, inverse, mixed_grad, *packs_a,
        ),
    )

    count = len(ff_swap)
    hidden_grad, token_grad, far_part, own_half, far_half, *got = together(
        hidden_grad, token_grad, far_part, *self_outs, *ff_swap, cross_swap, *enc_swap
    )
    ff_got, cross_swap, enc_swap = got[:count], got[count], got[count + 1 :]
    self_got = w_flip(far_half, 1, depth)
    ff_sum = add_all(ff_pieces[0], ff_got)
    ff_sp = swap_sp(ff_sum, sp)
    cross_pieces = [cross_half[0][d] + cross_swap[d].astype(F32) for d in range(depth)]
    cross_got = swap_z(cross_pieces, depth)
    self_half = [own_half[y].astype(F32) + self_got[y].astype(F32) for y in range(2)]
    self_swap = w_flip(self_half[1].astype(BF16), 2, depth)
    self_pieces = [self_half[0][d] + self_swap[d].astype(F32) for d in range(depth)]
    cross_sum = add_all(cross_pieces[0], [after(piece, self_swap) for piece in cross_got])
    self_more = swap_z(self_pieces, depth)
    cross_sp = swap_sp(cross_sum, sp)
    self_sum = add_all(self_pieces[0], self_more)
    self_sp = swap_sp(self_sum, sp)

    shift_back = (local - far) // BLK
    for r in range(1, sp):
        got = shift(far_part[r - 1], "sp", -r, sp)
        spec = pl.BlockSpec(
            (1, BLK, width), lambda s, i, spot: (s, i + jnp.where(spot[0] == 0, shift_back, 0), 0)
        )
        (token_grad,) = call(
            settle_kernel, (seqs, far // BLK), 1,
            [spec, pl.BlockSpec((1, BLK, width), lambda s, i, spot: (s, i, 0))],
            [spec], [((seqs, local, width), F32)], [], 2000.0, (spot, token_grad, got), {1: 0},
        )
    encoder_grad = own_enc_part
    for r in range(1, sp):
        encoder_grad = encoder_grad + enc_swap[r - 1].astype(F32)

    ff_total = add_all(ff_sum, ff_sp)
    cross_total = add_all(cross_sum, cross_sp)
    self_total = add_all(self_sum, self_sp)
    inner_total = jnp.concatenate([ff_total[c * shard : (c + 1) * shard] for c in range(chunks)], axis=1)
    outer_total = ff_total[chunks * shard :]
    small = cross_total[5 * shard :]
    cut = lambda total, k: total[k * shard : (k + 1) * shard]
    vec = lambda k: lax.dynamic_slice(small, (k, mine * shard), (1, shard))[0]
    bias_total = lax.dynamic_slice(small[8 : 8 + chunks].reshape(-1), (mine * bias_rows,), (bias_rows,))
    return (
        layer_out, hidden_grad, token_grad, encoder_grad,
        cut(self_total, 0), cut(self_total, 1), cut(self_total, 2), cut(cross_total, 0),
        cut(cross_total, 1), cut(cross_total, 2), cut(cross_total, 3), cut(cross_total, 4),
        inner_total, bias_total, outer_total, vec(4), vec(5), vec(6), vec(0), vec(1), vec(2), vec(3),
    )


def solution(mesh):
    tokens, table, vector = P("fsdp", "sp", None), P("fsdp", None), P("fsdp")
    order = P("fsdp", None, None)
    return jax.shard_map(
        functools.partial(on_device, mesh.shape["sp"], mesh.shape["fsdp"]),
        mesh=mesh,
        in_specs=(tokens,) * 4
        + (table, order, order)
        + (table,) * 9
        + (vector, table)
        + (vector,) * 7,
        out_specs=(tokens,) * 4 + (table,) * 9 + (vector, table) + (vector,) * 7,
        check_vma=False,
    )
```

time: 688 us -> 457 us (0.66)
  waiting for transfers between devices: 341 us -> 48.9 us
  starting transfers between devices: 11.8 us -> 61.2 us
  Pallas kernels: 272 us -> 303 us
  between operations: 14.5 us -> 1.7 us
  local copies, waits for them, and re-layouts: 21.2 us -> 12.3 us
    reduce_scatter x4 -> x0, waiting for transfers between devices: 201 us -> none  [reduce(): mine = lax.psum_scatter(grads, 'fsdp', scatter_dimension=0, tiled=True)[0]]
    all_gather x3 -> x0, waiting for transfers between devices: 60.8 us -> none  [gather(): return lax.all_gather(packed, 'fsdp', axis=0, tiled=False)]
    ppermute x8 -> x7, waiting for transfers between devices: 78.9 us -> 20.8 us  [shift(): lax.ppermute(array, axis, [((i + by) % size, i) for i in range(size)])]
    ppermute x0 -> x34, starting transfers between devices: none -> 52.8 us  [the longest x18 31.7 us: z_shift(): return lax.ppermute(array, 'fsdp', pairs)]
    pallas_call x4 -> x6, Pallas kernels: 272 us -> 303 us  [call(): pl.pallas_call(body, grid_spec=pltpu.PrefetchScalarGridSpec(num_scalar_pr...]
    ppermute x0 -> x34, waiting for transfers between devices: none -> 28.1 us  [the longest x18 14.7 us: z_shift(): return lax.ppermute(array, 'fsdp', pairs)]
  transfers between devices with their start and end apart: 15 -> 41, of which waited for: 10 -> 10; matrix products, arithmetic and copies ran while one was open for 3% -> 6% of each run, Pallas kernels for 9% -> 53%
where the time goes in v2:
time: 457 us; the launch traced here: 449 us
  Pallas kernels  303 us (66%)
  starting transfers between devices  61.2 us (13%)
  waiting for transfers between devices  48.9 us (11%)
  other arithmetic  21.3 us (5%)
  local copies, waits for them, and re-layouts  12.3 us (3%)
    pallas_call x6, Pallas kernels, call(): pl.pallas_call(body, grid_spec=pltpu.PrefetchScalarGridSpec(num_scalar_pr...  303 us
    ppermute x18, starting transfers between devices, z_shift(): return lax.ppermute(array, 'fsdp', pairs)  31.7 us
    ppermute x16, starting transfers between devices, w_flip(): lax.ppermute(array, 'fsdp', [(z * 4 + (w ^ mask), z * 4 + w) for z in ran...  21.1 us
    ppermute x7, waiting for transfers between devices, shift(): lax.ppermute(array, axis, [((i + by) % size, i) for i in range(size)])  20.8 us
    ppermute x18, waiting for transfers between devices, z_shift(): return lax.ppermute(array, 'fsdp', pairs)  14.7 us
    ppermute x16, waiting for transfers between devices, w_flip(): lax.ppermute(array, 'fsdp', [(z * 4 + (w ^ mask), z * 4 + w) for z in ran...  13.4 us
  transfers between devices with their start and end apart: 41, of which 10 were waited for; matrix products, arithmetic and copies ran while one was open for 6% of the time, Pallas kernels for 53%

profile of v2, /device:TPU:0, one launch (start us, length us, event | category | flops | bytes accessed | tf_op | source)
XLA Modules:
  0.0 448.6 jit_solution(3983940117657918218)
XLA Ops:
  3.2 5.0 %collective-permute-start = (bf16[96,512]{1,0:T(8,128)(2,1)S(1)}, bf16[96,512]{1,0:T(8,128)(2,1)S(1)}, u32[]{:S(2)}, u32[]{:S(2)}) collective-permute-start(bf16[96,512]{1,0:T(8,128)(2,1)S(1)} %constant_dynamic-update-slice_fusion.6), channel_id=1, source_target_pairs={{8,0},{10,2},{12,4},{14,6},{16,8},{18,10},{20,12},{22,14},{24,16},... | collective-permute-start | bytes 294920 | tf_op jit(solution)/shard_map/ppermute | solution.py:569
  9.2 1.5 constant_dynamic-slice_fusion
  10.8 1.6 collective-permute-start.7
  12.7 4.3 collective-permute-done.1
  17.0 2.3 collective-permute-start.4
  19.6 3.6 collective-permute-start.3
  25.3 6.0 %collective-permute-done.4 = bf16[176,512]{1,0:T(8,128)(2,1)S(1)} collective-permute-done((bf16[176,512]{1,0:T(8,128)(2,1)S(1)}, bf16[176,512]{1,0:T(8,128)(2,1)S(1)}, u32[]{:S(2)}, u32[]{:S(2)}) %collective-permute-start.4) | collective-permute-done | bytes 180256 | tf_op jit(solution)/shard_map/ppermute | solution.py:569
  37.4 2.2 collective-permute-start.13
  39.6 2.4 collective-permute-start.14
  42.0 4.3 collective-permute-done.7
  46.2 2.5 collective-permute-start.15
  52.5 56.7 %shard_map.408 = (bf16[2,512,2048]{2,1,0:T(8,128)(2,1)}, bf16[2,512,2048]{2,1,0:T(8,128)(2,1)}, bf16[2,512,1024]{2,1,0:T(8,128)(2,1)}, bf16[2,512,1024]{2,1,0:T(...) custom-call(s32[2,8]{1,0:T(2,128)} %docs.3, s32[4]{0:T(128)} %pad_add_fusion.spot, ...), custom_call_target="tpu_custom_call" | custom-call | flops 31999999868928 | bytes 16777216 | tf_op jit(solution)/shard_map/pallas_call | solution.py:547
  109.2 7.4 %collective-permute-start.16 = (bf16[4,176,512]{2,1,0:T(8,128)(2,1)}, bf16[4,176,512]{2,1,0:T(8,128)(2,1)S(1)}, u32[]{:S(2)}, u32[]{:S(2)}) collective-permute-start(bf16[4,176,512]{2,1,0:T(8,128)(2,1)} %collective-permute-done.12.pack2), channel_id=1, source_target_pairs={{2,0},{0,2},{6,4},{4,6},{10,8},{8,10},{14,12},{12,14},{18,16},{16,... | collective-permute-start | bytes 2162696 | tf_op jit(solution)/shard_map/ppermute | solution.py:573
  116.6 2.3 pad_maximum_fusion.pack0
  119.9 74.6 %shard_map.409 = (bf16[2,512,1024]{2,1,0:T(8,128)(2,1)}, bf16[2,512,1024]{2,1,0:T(8,128)(2,1)}, bf16[2,512,1024]{2,1,0:T(8,128)(2,1)}, bf16[2,512,1024]{2,1,0:T(...) custom-call(s32[4]{0:T(128)} %pad_add_fusion.spot, ...), custom_call_target="tpu_custom_call" | custom-call | flops 31999999868928 | bytes 16777216 | tf_op jit(solution)/shard_map/pallas_call | solution.py:547
  195.1 2.8 collective-permute-done.18.pack1
  199.1 59.1 %shard_map.410 = (f32[2,512,1024]{2,1,0:T(8,128)}, f32[2,1024,512]{2,1,0:T(8,128)}, bf16[4,256,512]{2,1,0:T(8,128)(2,1)}, bf16[4,256,512]{2,1,0:T(8,128)(2,1)}, ...) custom-call(s32[4]{0:T(128)} %pad_add_fusion.spot, ...), custom_call_target="tpu_custom_call" | custom-call | flops 70000001941504 | bytes 16777216 | tf_op jit(solution)/shard_map/pallas_call | solution.py:547
  258.3 1.7 collective-permute-start.21
  260.1 57.7 %shard_map.411 = (f32[2,512,1024]{2,1,0:T(8,128)}, bf16[2,512,1024]{2,1,0:T(8,128)(2,1)}, f32[2,512,512]{2,1,0:T(8,128)}, bf16[1,2,512,512]{3,2,1,0:T(8,128)(2,1...) custom-call(s32[4]{0:T(128)} %pad_add_fusion.spot, ...), custom_call_target="tpu_custom_call" | custom-call | flops 55999998197760 | bytes 16777216 | tf_op jit(solution)/shard_map/pallas_call | solution.py:547
  319.6 2.0 add_bitcast_fusion.5
  321.6 2.9 add_bitcast_fusion.2
  328.6 2.5 collective-permute-start.26
  331.1 48.9 %shard_map.412 = (f32[2,1024,512]{2,1,0:T(8,128)}, f32[2,1024,512]{2,1,0:T(8,128)}, bf16[1,2,768,512]{3,2,1,0:T(8,128)(2,1)}, bf16[2,4,96,512]{3,2,1,0:T(8,128)(2,1)}, bf16[2,4,96,512]{3,2,1,0:T(8,128)(2,1)}) custom-call(s32[2,8]{1,0:T(2,128)} %docs.3, s32[4]{0:T(128)} %pad_add_fusion.spot, bf16[2,1024,512]{2,1,0:T(8,128)(2,1)} %hidden.4, ...), custom_call_target="tpu_custom_call" | custom-call | flops 50000000188416 | bytes 16777216 | tf_op jit(solution)/shard_map/pallas_call | solution.py:547
  382.9 6.5 %collective-permute-start.30 = (bf16[2,4,96,512]{3,2,1,0:T(8,128)(2,1)}, bf16[2,4,96,512]{3,2,1,0:T(8,128)(2,1)S(1)}, u32[]{:S(2)}, u32[]{:S(2)}) collective-permute-start(bf16[2,4,96,512]{3,2,1,0:T(8,128)(2,1)} %get-tuple-element.208), channel_id=1, source_target_pairs={{2,0},{0,2},{6,4},{4,6},{10,8},{8,10},{14,12},{12,14},{18,16},{16,... | collective-permute-start | bytes 2359304 | tf_op jit(solution)/shard_map/ppermute | solution.py:573
  391.1 3.5 collective-permute-start.38
  394.6 2.9 convert_add_fusion
  397.5 1.7 collective-permute-start.29
  402.3 9.4 %collective-permute-done.31 = bf16[4,96,512]{2,1,0:T(8,128)(2,1)S(1)} collective-permute-done((bf16[4,96,512]{2,1,0:T(8,128)(2,1)S(1)}, bf16[4,96,512]{2,1,0:T(8,128)(2,1)S(1)}, u32[]{:S(2)}, u32[]{:S(2)}) %collective-permute-start.31) | collective-permute-done | bytes 393248 | tf_op jit(solution)/shard_map/ppermute | solution.py:573
  413.6 2.8 collective-permute-start.34
  419.0 2.1 collective-permute-done.33
  421.7 16.5 %collective-permute-done.39 = bf16[176,512]{1,0:T(8,128)(2,1)S(1)} collective-permute-done((bf16[176,512]{1,0:T(8,128)(2,1)S(1)}, bf16[176,512]{1,0:T(8,128)(2,1)S(1)}, u32[]{:S(2)}, u32[]{:S(2)}) %collective-permute-start.39) | collective-permute-done | bytes 180256 | tf_op jit(solution)/shard_map/ppermute | solution.py:564
  442.0 6.2 %shard_map.413 = f32[2,1024,512]{2,1,0:T(8,128)} custom-call(s32[4]{0:T(128)} %pad_add_fusion.spot, f32[2,1024,512]{2,1,0:T(8,128)} %get-tuple-element.203.own, bf16[2,768,512]{2,1,0:T(8,128)(2,1)} %collective-permute-done.29.far), custom_call_target="tpu_custom_call", output_to_operand_aliasing={{}: (1, {})} | custom-call | flops 1999999991808 | bytes 16777216 | tf_op jit(solution)/shard_map/pallas_call | solution.py:547
  (160 shorter events, 40.9 us)
Async XLA Ops:
  3.2 9.5 %collective-permute-start = (bf16[96,512]{1,0:T(8,128)(2,1)S(1)}, bf16[96,512]{1,0:T(8,128)(2,1)S(1)}, u32[]{:S(2)}, u32[]{:S(2)}) collective-permute-start(bf16[96,512]{1,0:T(8,128)(2,1)S(1)} %constant_dynamic-update-slice_fusion.6), channel_id=1, source_target_pairs={{8,0},{10,2},{12,4},{14,6},{16,8},{18,10},{20,12},{22,14},{24,16},... | collective-permute-start | bytes 294920 | tf_op jit(solution)/shard_map/ppermute | solution.py:569
  10.8 35.5 %collective-permute-start.7 = (bf16[2,768,512]{2,1,0:T(8,128)(2,1)S(1)}, bf16[2,768,512]{2,1,0:T(8,128)(2,1)}, u32[]{:S(2)}, u32[]{:S(2)}) collective-permute-start(bf16[2,768,512]{2,1,0:T(8,128)(2,1)S(1)} %constant_dynamic-slice_fusion), channel_id=1, source_target_pairs={{1,0},{0,1},{3,2},{2,3},{5,4},{4,5},{7,6},{6,7},{9,8},{8,9},{11,10... | collective-permute-start | bytes 4718600 | tf_op jit(solution)/shard_map/ppermute | solution.py:564
  17.0 14.3 %collective-permute-start.4 = (bf16[176,512]{1,0:T(8,128)(2,1)S(1)}, bf16[176,512]{1,0:T(8,128)(2,1)S(1)}, u32[]{:S(2)}, u32[]{:S(2)}) collective-permute-start(bf16[176,512]{1,0:T(8,128)(2,1)S(1)} %constant_dynamic-update-slice_fusion), channel_id=1, source_target_pairs={{16,0},{18,2},{20,4},{22,6},{24,8},{26,10},{28,12},{30,14},{0,16},... | collective-permute-start | bytes 540680 | tf_op jit(solution)/shard_map/ppermute | solution.py:569
  19.4 12.0 %collective-permute-start.5 = (bf16[176,512]{1,0:T(8,128)(2,1)S(1)}, bf16[176,512]{1,0:T(8,128)(2,1)S(1)}, u32[]{:S(2)}, u32[]{:S(2)}) collective-permute-start(bf16[176,512]{1,0:T(8,128)(2,1)S(1)} %constant_dynamic-update-slice_fusion), channel_id=1, source_target_pairs={{24,0},{26,2},{28,4},{30,6},{0,8},{2,10},{4,12},{6,14},{8,16},{10,... | collective-permute-start | bytes 540680 | tf_op jit(solution)/shard_map/ppermute | solution.py:569
  19.6 13.0 %collective-permute-start.3 = (bf16[176,512]{1,0:T(8,128)(2,1)S(1)}, bf16[176,512]{1,0:T(8,128)(2,1)S(1)}, u32[]{:S(2)}, u32[]{:S(2)}) collective-permute-start(bf16[176,512]{1,0:T(8,128)(2,1)S(1)} %constant_dynamic-update-slice_fusion), channel_id=1, source_target_pairs={{8,0},{10,2},{12,4},{14,6},{16,8},{18,10},{20,12},{22,14},{24,16},... | collective-permute-start | bytes 540680 | tf_op jit(solution)/shard_map/ppermute | solution.py:569
  23.8 11.5 %collective-permute-start.9 = (bf16[4,96,512]{2,1,0:T(8,128)(2,1)S(1)}, bf16[4,96,512]{2,1,0:T(8,128)(2,1)S(1)}, u32[]{:S(2)}, u32[]{:S(2)}) collective-permute-start(bf16[4,96,512]{2,1,0:T(8,128)(2,1)S(1)} %pad_maximum_fusion.2.pack0), channel_id=1, source_target_pairs={{4,0},{6,2},{0,4},{2,6},{12,8},{14,10},{8,12},{10,14},{20,16},{22,... | collective-permute-start | bytes 1179656 | tf_op jit(solution)/shard_map/ppermute | solution.py:573
  34.8 13.9 %collective-permute-start.8 = (bf16[4,96,512]{2,1,0:T(8,128)(2,1)S(1)}, bf16[4,96,512]{2,1,0:T(8,128)(2,1)S(1)}, u32[]{:S(2)}, u32[]{:S(2)}) collective-permute-start(bf16[4,96,512]{2,1,0:T(8,128)(2,1)S(1)} %pad_maximum_fusion.2.pack0), channel_id=1, source_target_pairs={{2,0},{0,2},{6,4},{4,6},{10,8},{8,10},{14,12},{12,14},{18,16},{16,... | collective-permute-start | bytes 1179656 | tf_op jit(solution)/shard_map/ppermute | solution.py:573
  35.4 14.9 %collective-permute-start.10 = (bf16[4,96,512]{2,1,0:T(8,128)(2,1)S(1)}, bf16[4,96,512]{2,1,0:T(8,128)(2,1)S(1)}, u32[]{:S(2)}, u32[]{:S(2)}) collective-permute-start(bf16[4,96,512]{2,1,0:T(8,128)(2,1)S(1)} %collective-permute-done.9.pack2), channel_id=1, source_target_pairs={{2,0},{0,2},{6,4},{4,6},{10,8},{8,10},{14,12},{12,14},{18,16},{16,... | collective-permute-start | bytes 1179656 | tf_op jit(solution)/shard_map/ppermute | solution.py:573
  37.4 71.8 %collective-permute-start.13 = (bf16[256,512]{1,0:T(8,128)(2,1)}, bf16[256,512]{1,0:T(8,128)(2,1)}, u32[]{:S(2)}, u32[]{:S(2)}) collective-permute-start(bf16[256,512]{1,0:T(8,128)(2,1)} %constant_dynamic-update-slice_fusion.9), channel_id=1, source_target_pairs={{8,0},{10,2},{12,4},{14,6},{16,8},{18,10},{20,12},{22,14},{24,16},... | collective-permute-start | bytes 786440 | tf_op jit(solution)/shard_map/ppermute | solution.py:569
  39.6 69.6 %collective-permute-start.14 = (bf16[256,512]{1,0:T(8,128)(2,1)}, bf16[256,512]{1,0:T(8,128)(2,1)}, u32[]{:S(2)}, u32[]{:S(2)}) collective-permute-start(bf16[256,512]{1,0:T(8,128)(2,1)} %constant_dynamic-update-slice_fusion.9), channel_id=1, source_target_pairs={{16,0},{18,2},{20,4},{22,6},{24,8},{26,10},{28,12},{30,14},{0,16},... | collective-permute-start | bytes 786440 | tf_op jit(solution)/shard_map/ppermute | solution.py:569
  46.2 63.0 %collective-permute-start.15 = (bf16[256,512]{1,0:T(8,128)(2,1)}, bf16[256,512]{1,0:T(8,128)(2,1)}, u32[]{:S(2)}, u32[]{:S(2)}) collective-permute-start(bf16[256,512]{1,0:T(8,128)(2,1)} %constant_dynamic-update-slice_fusion.9), channel_id=1, source_target_pairs={{24,0},{26,2},{28,4},{30,6},{0,8},{2,10},{4,12},{6,14},{8,16},{10,... | collective-permute-start | bytes 786440 | tf_op jit(solution)/shard_map/ppermute | solution.py:569
  48.7 60.5 %collective-permute-start.12 = (bf16[4,176,512]{2,1,0:T(8,128)(2,1)}, bf16[4,176,512]{2,1,0:T(8,128)(2,1)}, u32[]{:S(2)}, u32[]{:S(2)}) collective-permute-start(bf16[4,176,512]{2,1,0:T(8,128)(2,1)} %pad_maximum_fusion.1.pack0), channel_id=1, source_target_pairs={{4,0},{6,2},{0,4},{2,6},{12,8},{14,10},{8,12},{10,14},{20,16},{22,... | collective-permute-start | bytes 2162696 | tf_op jit(solution)/shard_map/ppermute | solution.py:573
  51.0 58.2 %collective-permute-start.11 = (bf16[2,512,512]{2,1,0:T(8,128)(2,1)}, bf16[2,512,512]{2,1,0:T(8,128)(2,1)}, u32[]{:S(2)}, u32[]{:S(2)}) collective-permute-start(bf16[2,512,512]{2,1,0:T(8,128)(2,1)} %own_enc.3), channel_id=1, source_target_pairs={{1,0},{0,1},{3,2},{2,3},{5,4},{4,5},{7,6},{6,7},{9,8},{8,9},{11,10... | collective-permute-start | bytes 3145736 | tf_op jit(solution)/shard_map/ppermute | solution.py:564
  109.2 9.7 %collective-permute-start.16 = (bf16[4,176,512]{2,1,0:T(8,128)(2,1)}, bf16[4,176,512]{2,1,0:T(8,128)(2,1)S(1)}, u32[]{:S(2)}, u32[]{:S(2)}) collective-permute-start(bf16[4,176,512]{2,1,0:T(8,128)(2,1)} %collective-permute-done.12.pack2), channel_id=1, source_target_pairs={{2,0},{0,2},{6,4},{4,6},{10,8},{8,10},{14,12},{12,14},{18,16},{16,... | collective-permute-start | bytes 2162696 | tf_op jit(solution)/shard_map/ppermute | solution.py:573
  118.9 75.5 %collective-permute-start.17 = (bf16[4,256,512]{2,1,0:T(8,128)(2,1)}, bf16[4,256,512]{2,1,0:T(8,128)(2,1)}, u32[]{:S(2)}, u32[]{:S(2)}) collective-permute-start(bf16[4,256,512]{2,1,0:T(8,128)(2,1)} %pad_maximum_fusion.pack0), channel_id=1, source_target_pairs={{4,0},{6,2},{0,4},{2,6},{12,8},{14,10},{8,12},{10,14},{20,16},{22,... | collective-permute-start | bytes 3145736 | tf_op jit(solution)/shard_map/ppermute | solution.py:573
  258.1 59.7 %collective-permute-start.20 = (bf16[4,256,512]{2,1,0:T(8,128)(2,1)}, bf16[4,256,512]{2,1,0:T(8,128)(2,1)}, u32[]{:S(2)}, u32[]{:S(2)}) collective-permute-start(bf16[4,256,512]{2,1,0:T(8,128)(2,1)} %get-tuple-element.175), channel_id=1, source_target_pairs={{2,0},{0,2},{6,4},{4,6},{10,8},{8,10},{14,12},{12,14},{18,16},{16,... | collective-permute-start | bytes 3145736 | tf_op jit(solution)/shard_map/ppermute | solution.py:573
  258.3 59.5 %collective-permute-start.21 = (bf16[4,256,512]{2,1,0:T(8,128)(2,1)}, bf16[4,256,512]{2,1,0:T(8,128)(2,1)}, u32[]{:S(2)}, u32[]{:S(2)}) collective-permute-start(bf16[4,256,512]{2,1,0:T(8,128)(2,1)} %get-tuple-element.176), channel_id=1, source_target_pairs={{4,0},{6,2},{0,4},{2,6},{12,8},{14,10},{8,12},{10,14},{20,16},{22,... | collective-permute-start | bytes 3145736 | tf_op jit(solution)/shard_map/ppermute | solution.py:573
  260.0 57.8 %collective-permute-start.22 = (bf16[4,256,512]{2,1,0:T(8,128)(2,1)}, bf16[4,256,512]{2,1,0:T(8,128)(2,1)}, u32[]{:S(2)}, u32[]{:S(2)}) collective-permute-start(bf16[4,256,512]{2,1,0:T(8,128)(2,1)} %get-tuple-element.177), channel_id=1, source_target_pairs={{6,0},{4,2},{2,4},{0,6},{14,8},{12,10},{10,12},{8,14},{22,16},{20,... | collective-permute-start | bytes 3145736 | tf_op jit(solution)/shard_map/ppermute | solution.py:573
  318.3 61.8 %collective-permute-start.28 = (bf16[2,512,512]{2,1,0:T(8,128)(2,1)}, bf16[2,512,512]{2,1,0:T(8,128)(2,1)}, u32[]{:S(2)}, u32[]{:S(2)}) collective-permute-start(bf16[2,512,512]{2,1,0:T(8,128)(2,1)} %bitcast.135), channel_id=1, source_target_pairs={{1,0},{0,1},{3,2},{2,3},{5,4},{4,5},{7,6},{6,7},{9,8},{8,9},{11,10... | collective-permute-start | bytes 3145736 | tf_op jit(solution)/shard_map/ppermute | solution.py:564
  326.8 53.3 %collective-permute-start.27 = (bf16[4,176,512]{2,1,0:T(8,128)(2,1)}, bf16[4,176,512]{2,1,0:T(8,128)(2,1)}, u32[]{:S(2)}, u32[]{:S(2)}) collective-permute-start(bf16[4,176,512]{2,1,0:T(8,128)(2,1)} %add_bitcast_fusion), channel_id=1, source_target_pairs={{4,0},{6,2},{0,4},{2,6},{12,8},{14,10},{8,12},{10,14},{20,16},{22,... | collective-permute-start | bytes 2162696 | tf_op jit(solution)/shard_map/ppermute | solution.py:573
  327.3 52.8 %collective-permute-start.24 = (bf16[256,512]{1,0:T(8,128)(2,1)}, bf16[256,512]{1,0:T(8,128)(2,1)}, u32[]{:S(2)}, u32[]{:S(2)}) collective-permute-start(bf16[256,512]{1,0:T(8,128)(2,1)} %get-tuple-element.197), channel_id=1, source_target_pairs={{24,0},{26,2},{28,4},{30,6},{0,8},{2,10},{4,12},{6,14},{8,16},{10,... | collective-permute-start | bytes 786440 | tf_op jit(solution)/shard_map/ppermute | solution.py:569
  327.3 52.8 %collective-permute-start.25 = (bf16[256,512]{1,0:T(8,128)(2,1)}, bf16[256,512]{1,0:T(8,128)(2,1)}, u32[]{:S(2)}, u32[]{:S(2)}) collective-permute-start(bf16[256,512]{1,0:T(8,128)(2,1)} %get-tuple-element.198), channel_id=1, source_target_pairs={{16,0},{18,2},{20,4},{22,6},{24,8},{26,10},{28,12},{30,14},{0,16},... | collective-permute-start | bytes 786440 | tf_op jit(solution)/shard_map/ppermute | solution.py:569
  328.6 51.5 %collective-permute-start.26 = (bf16[256,512]{1,0:T(8,128)(2,1)}, bf16[256,512]{1,0:T(8,128)(2,1)}, u32[]{:S(2)}, u32[]{:S(2)}) collective-permute-start(bf16[256,512]{1,0:T(8,128)(2,1)} %get-tuple-element.199), channel_id=1, source_target_pairs={{8,0},{10,2},{12,4},{14,6},{16,8},{18,10},{20,12},{22,14},{24,16},... | collective-permute-start | bytes 786440 | tf_op jit(solution)/shard_map/ppermute | solution.py:569
  381.5 15.9 %collective-permute-start.40 = (bf16[256,512]{1,0:T(8,128)(2,1)S(1)}, bf16[256,512]{1,0:T(8,128)(2,1)S(1)}, u32[]{:S(2)}, u32[]{:S(2)}) collective-permute-start(bf16[256,512]{1,0:T(8,128)(2,1)S(1)} %fusion.20), channel_id=1, source_target_pairs={{1,0},{0,1},{3,2},{2,3},{5,4},{4,5},{7,6},{6,7},{9,8},{8,9},{11,10... | collective-permute-start | bytes 786440 | tf_op jit(solution)/shard_map/ppermute | solution.py:564
  382.9 18.3 %collective-permute-start.30 = (bf16[2,4,96,512]{3,2,1,0:T(8,128)(2,1)}, bf16[2,4,96,512]{3,2,1,0:T(8,128)(2,1)S(1)}, u32[]{:S(2)}, u32[]{:S(2)}) collective-permute-start(bf16[2,4,96,512]{3,2,1,0:T(8,128)(2,1)} %get-tuple-element.208), channel_id=1, source_target_pairs={{2,0},{0,2},{6,4},{4,6},{10,8},{8,10},{14,12},{12,14},{18,16},{16,... | collective-permute-start | bytes 2359304 | tf_op jit(solution)/shard_map/ppermute | solution.py:573
  390.7 11.6 %collective-permute-start.36 = (bf16[176,512]{1,0:T(8,128)(2,1)S(1)}, bf16[176,512]{1,0:T(8,128)(2,1)S(1)}, u32[]{:S(2)}, u32[]{:S(2)}) collective-permute-start(bf16[176,512]{1,0:T(8,128)(2,1)S(1)} %get-tuple-element.221), channel_id=1, source_target_pairs={{24,0},{26,2},{28,4},{30,6},{0,8},{2,10},{4,12},{6,14},{8,16},{10,... | collective-permute-start | bytes 540680 | tf_op jit(solution)/shard_map/ppermute | solution.py:569
  390.8 20.9 %collective-permute-start.37 = (bf16[176,512]{1,0:T(8,128)(2,1)S(1)}, bf16[176,512]{1,0:T(8,128)(2,1)S(1)}, u32[]{:S(2)}, u32[]{:S(2)}) collective-permute-start(bf16[176,512]{1,0:T(8,128)(2,1)S(1)} %get-tuple-element.223), channel_id=1, source_target_pairs={{16,0},{18,2},{20,4},{22,6},{24,8},{26,10},{28,12},{30,14},{0,16},... | collective-permute-start | bytes 540680 | tf_op jit(solution)/shard_map/ppermute | solution.py:569
  391.1 20.6 %collective-permute-start.38 = (bf16[176,512]{1,0:T(8,128)(2,1)S(1)}, bf16[176,512]{1,0:T(8,128)(2,1)S(1)}, u32[]{:S(2)}, u32[]{:S(2)}) collective-permute-start(bf16[176,512]{1,0:T(8,128)(2,1)S(1)} %get-tuple-element.222), channel_id=1, source_target_pairs={{8,0},{10,2},{12,4},{14,6},{16,8},{18,10},{20,12},{22,14},{24,16},... | collective-permute-start | bytes 540680 | tf_op jit(solution)/shard_map/ppermute | solution.py:569
  397.5 44.5 %collective-permute-start.29 = (bf16[2,768,512]{2,1,0:T(8,128)(2,1)S(1)}, bf16[2,768,512]{2,1,0:T(8,128)(2,1)}, u32[]{:S(2)}, u32[]{:S(2)}) collective-permute-start(bf16[2,768,512]{2,1,0:T(8,128)(2,1)S(1)} %bitcast.134), channel_id=1, source_target_pairs={{1,0},{0,1},{3,2},{2,3},{5,4},{4,5},{7,6},{6,7},{9,8},{8,9},{11,10... | collective-permute-start | bytes 4718600 | tf_op jit(solution)/shard_map/ppermute | solution.py:564
  401.4 10.2 %collective-permute-start.31 = (bf16[4,96,512]{2,1,0:T(8,128)(2,1)S(1)}, bf16[4,96,512]{2,1,0:T(8,128)(2,1)S(1)}, u32[]{:S(2)}, u32[]{:S(2)}) collective-permute-start(bf16[4,96,512]{2,1,0:T(8,128)(2,1)S(1)} %get-tuple-element.224), channel_id=1, source_target_pairs={{4,0},{6,2},{0,4},{2,6},{12,8},{14,10},{8,12},{10,14},{20,16},{22,... | collective-permute-start | bytes 1179656 | tf_op jit(solution)/shard_map/ppermute | solution.py:573
  417.5 20.7 %collective-permute-start.39 = (bf16[176,512]{1,0:T(8,128)(2,1)S(1)}, bf16[176,512]{1,0:T(8,128)(2,1)S(1)}, u32[]{:S(2)}, u32[]{:S(2)}) collective-permute-start(bf16[176,512]{1,0:T(8,128)(2,1)S(1)} %fusion.22), channel_id=1, source_target_pairs={{1,0},{0,1},{3,2},{2,3},{5,4},{4,5},{7,6},{6,7},{9,8},{8,9},{11,10... | collective-permute-start | bytes 540680 | tf_op jit(solution)/shard_map/ppermute | solution.py:564
  421.2 20.0 %collective-permute-start.35 = (bf16[96,512]{1,0:T(8,128)(2,1)S(1)}, bf16[96,512]{1,0:T(8,128)(2,1)S(1)}, u32[]{:S(2)}, u32[]{:S(2)}) collective-permute-start(bf16[96,512]{1,0:T(8,128)(2,1)S(1)} %fusion.21), channel_id=1, source_target_pairs={{1,0},{0,1},{3,2},{2,3},{5,4},{4,5},{7,6},{6,7},{9,8},{8,9},{11,10... | collective-permute-start | bytes 294920 | tf_op jit(solution)/shard_map/ppermute | solution.py:564
  (38 other events, 525.9 us)
